TPU v7x, 256 devices: a whole 4x4x8 slice. The times are simulated.
256 devices in a mesh: head: 64 (over z_hi, x, y, core), mb: 4 (over z_lo).
Axes of the slice: x: 4, y: 4, z: 8 (z_hi: 2, z_lo: 4; z = z_hi * 4 + z_lo), core: 2. Of those that a mesh axis runs over, the one named last changes fastest.
Arguments:
- arrivals: bfloat16 [4, 64, 128, 4096], P('mb', 'head'), may hold values from -6 to 6
- owners: int32 [4], P('mb'), may hold values from 0 to 63
- doc_lengths: int32 [4, 4], P('mb'), may hold values from 1 to 64, 128 in all within a row
- w_in: bfloat16 [4096, 2, 8192], P(None, None, 'head'), may hold values from -0.09375 to 0.09375
- w_bc: bfloat16 [2048, 4096], P('head'), may hold values from -0.09375 to 0.09375
- w_dt: bfloat16 [128, 4096], P('head'), may hold values from -0.09375 to 0.09375
- conv_x: float32 [4, 8192], P(None, 'head'), may hold values from -3 to 3
- conv_bc: float32 [4, 2048], P(None, 'head'), may hold values from -3 to 3
- dt_bias: float32 [128], P('head'), may hold values from -3 to -1
- a_log: float32 [128], P('head'), may hold values from -3.2 to -0.9
- skip_scale: float32 [128], P('head'), may hold values from 0.5 to 2
- norm_gain: float32 [8192], P('head'), may hold values from 0.1 to 1.9
- w_out: bfloat16 [8192, 4096], P('head'), may hold values from -0.0625 to 0.0625
- out_grad: bfloat16 [4, 128, 4096], P('mb', 'head'), may hold values from -6 to 6
Outputs:
- layer_out: bfloat16 [4, 128, 4096], P('mb', 'head')
- in_grad: bfloat16 [4, 128, 4096], P('mb', 'head')
- grad_w_in: bfloat16 [4096, 2, 8192], P('mb', None, 'head')
- grad_w_bc: bfloat16 [4096, 2048], P('mb', 'head')
- grad_w_dt: bfloat16 [4096, 128], P('mb', 'head')
- grad_w_out: bfloat16 [4096, 8192], P('mb', 'head')
Inputs may be any that keep to these rules, and one draw needn't show every extreme that they name: `doc_lengths`: each row sums to 128; the longest document of each row has exactly 64 positions. owners[m] is an index along head.
All inputs are finite; a program needn't handle non-finite values.
Results may differ from a plain program's by a relative error of at most 0.014.
Values may be sent and summed in bfloat16 or wider, within the bound.
A program may use at most 64 MiB of HBM per device.

v0:
```python
import jax
import jax.numpy as jnp
from jax import lax
from jax.sharding import PartitionSpec as P

STATE = 128
G = 8


epsilon = 1e-05
highest = lax.Precision.HIGHEST


def spread_2(value, axis, source):
    kept = jnp.where(lax.axis_index(axis) == source, value, 0).astype(value.dtype)
    return lax.psum(kept, axis)


def doc_index(doc_lengths, length):
    ends = jnp.cumsum(doc_lengths, dtype=jnp.int32)
    places = jnp.arange(length, dtype=jnp.int32)
    return jnp.sum((places[:, None] >= ends[None, :]).astype(jnp.int32), axis=1, dtype=jnp.int32)


def conv_reset(values, kernel, doc_ids):
    taps = kernel.shape[0]
    result = values * kernel[taps - 1][None, :]
    for offset in range(1, taps):
        shifted = jnp.concatenate(
            [jnp.zeros((offset, values.shape[1]), values.dtype), values[:-offset]], axis=0
        )
        same_doc = jnp.concatenate(
            [jnp.zeros((offset,), jnp.bool_), doc_ids[offset:] == doc_ids[:-offset]]
        )
        result = (
            result
            + jnp.where(same_doc[:, None], shifted, jnp.zeros_like(shifted))
            * kernel[taps - 1 - offset][None, :]
        )
    return result


def state_mix(per_head, step_size, rates, b_heads, c_heads, doc_ids):
    length = per_head.shape[0]
    cumulative = jnp.cumsum(step_size * rates[None, :], axis=0)
    places = jnp.arange(length, dtype=jnp.int32)
    visible = (places[:, None] >= places[None, :]) & (doc_ids[:, None] == doc_ids[None, :])
    log_gaps = cumulative.T[:, :, None] - cumulative.T[:, None, :]
    safe_gaps = jnp.where(visible[None], log_gaps, jnp.zeros_like(log_gaps))
    decays = jnp.where(visible[None], jnp.exp(safe_gaps), jnp.zeros_like(log_gaps))
    scores = jnp.einsum("thn,shn->hts", c_heads, b_heads, precision=highest)
    inputs_scaled = per_head * step_size[:, :, None]
    return jnp.einsum("hts,shp->thp", scores * decays, inputs_scaled, precision=highest)


def head_part(projected, b_heads, c_heads, dt_raw, conv_x, dt_bias, a_log, skip_scale, doc_ids):
    length = projected.shape[0]
    channels = projected.shape[1] // 2
    head_count = dt_raw.shape[1]
    conv_out = jax.nn.silu(conv_reset(projected[:, :channels], conv_x, doc_ids))
    step_size = jax.nn.softplus(dt_raw + dt_bias[None, :])
    rates = -jnp.exp(a_log)
    per_head = conv_out.reshape(length, head_count, channels // head_count)
    mixed_state = (
        state_mix(per_head, step_size, rates, b_heads, c_heads, doc_ids)
        + skip_scale[None, :, None] * per_head
    )
    return mixed_state.reshape(length, channels) * jax.nn.silu(projected[:, channels:])


def group_total(partial_value, group_mask):
    totals = lax.psum(partial_value[:, None] * group_mask[None, :], "head")
    return jnp.sum(totals * group_mask[None, :], axis=1)


def per_device(
    arrivals,
    owners,
    doc_lengths,
    w_in,
    w_bc,
    w_dt,
    conv_x,
    conv_bc,
    dt_bias,
    a_log,
    skip_scale,
    norm_gain,
    w_out,
    out_grad,
):
    devices = lax.axis_size("head")
    my_index = lax.axis_index("head")
    arrived = arrivals[0, 0]
    length, model_width = arrived.shape
    features = spread_2(arrived, "head", owners[0])
    doc_ids = doc_index(doc_lengths[0], length)
    head_count = w_dt.shape[0]
    channels = w_in.shape[2]
    w_flat = w_in.reshape(model_width, 2 * channels)
    contract = (((1,), (1,)), ((), ()))
    columns = (((0,), (0,)), ((), ()))
    projected = jnp.dot(features, w_flat, preferred_element_type=jnp.float32)
    state_pre = lax.dot_general(features, w_bc, contract, preferred_element_type=jnp.float32)
    dt_raw = lax.dot_general(features, w_dt, contract, preferred_element_type=jnp.float32)

    def state_local(values):
        return jax.nn.silu(conv_reset(values, conv_bc, doc_ids))

    state_act, state_back = jax.vjp(state_local, state_pre)
    state_all = lax.all_gather(state_act.astype(jnp.bfloat16), "head", axis=1, tiled=True)
    spread = G * STATE
    per_group = head_count * devices // G
    my_group = my_index * head_count // per_group
    b_cols = lax.dynamic_slice_in_dim(state_all, my_group * STATE, STATE, 1).astype(jnp.float32)
    c_cols = lax.dynamic_slice_in_dim(state_all, spread + my_group * STATE, STATE, 1).astype(
        jnp.float32
    )

    def gated_local(proj_in, b_in, c_in, raw_in):
        b_heads = jnp.broadcast_to(b_in[:, None, :], (length, head_count, STATE))
        c_heads = jnp.broadcast_to(c_in[:, None, :], (length, head_count, STATE))
        return head_part(
            proj_in, b_heads, c_heads, raw_in, conv_x, dt_bias, a_log, skip_scale, doc_ids
        )

    gated, gated_back = jax.vjp(gated_local, projected, b_cols, c_cols, dt_raw)
    group_mask = (jnp.arange(G, dtype=jnp.int32) == my_group).astype(jnp.float32)
    group_width = channels * devices // G
    squares = group_total(jnp.sum(gated * gated, axis=1), group_mask)
    inverse = lax.rsqrt(squares / group_width + epsilon)
    norm_gains = norm_gain[None, :]
    normed = (gated * inverse[:, None] * norm_gains).astype(jnp.bfloat16)
    block = normed
    layer_out = lax.psum_scatter(
        jnp.dot(block, w_out, preferred_element_type=jnp.float32),
        "head",
        scatter_dimension=0,
        tiled=True,
    ).astype(jnp.bfloat16)
    shard_rows = lax.all_gather(out_grad[0], "head", axis=0, tiled=True)
    block = lax.dot_general(shard_rows, w_out, contract, preferred_element_type=jnp.float32)
    d_normed = block
    grad_out = lax.dot_general(shard_rows, normed, columns, preferred_element_type=jnp.float32)
    d_normed, grad_out = (d_normed, grad_out)
    weighted = d_normed * norm_gains
    inner = group_total(jnp.sum(weighted * gated, axis=1), group_mask)
    d_gated = (
        inverse[:, None] * weighted
        - gated * (inverse * inverse * inverse * inner / group_width)[:, None]
    )
    d_proj, d_b, d_c, d_raw = gated_back(d_gated)
    d_state_all = jnp.zeros((length, 2 * spread), jnp.float32)
    d_state_all = lax.dynamic_update_slice_in_dim(d_state_all, d_b, my_group * STATE, 1)
    d_state_all = lax.dynamic_update_slice_in_dim(d_state_all, d_c, spread + my_group * STATE, 1)
    d_state_act = lax.psum_scatter(d_state_all, "head", scatter_dimension=1, tiled=True)
    (d_pre,) = state_back(d_state_act)
    d_proj = d_proj.astype(jnp.bfloat16)
    d_pre = d_pre.astype(jnp.bfloat16)
    d_raw = d_raw.astype(jnp.bfloat16)
    result = lax.dot_general(d_proj, w_flat, contract, preferred_element_type=jnp.float32)
    result = result + jnp.dot(d_pre, w_bc, preferred_element_type=jnp.float32)
    in_grad = lax.psum_scatter(
        result + jnp.dot(d_raw, w_dt, preferred_element_type=jnp.float32),
        "head",
        scatter_dimension=0,
        tiled=True,
    ).astype(jnp.bfloat16)
    grad_in = lax.dot_general(
        features, d_proj, columns, preferred_element_type=jnp.float32
    ).reshape(model_width, 2, channels)
    grad_bc = lax.dot_general(features, d_pre, columns, preferred_element_type=jnp.float32)
    grad_dt = lax.dot_general(features, d_raw, columns, preferred_element_type=jnp.float32)
    reduced = (
        lax.psum_scatter(
            grad_in.astype(jnp.bfloat16), "mb", scatter_dimension=0, tiled=True
        ).astype(jnp.float32),
        lax.psum_scatter(
            grad_bc.astype(jnp.bfloat16), "mb", scatter_dimension=0, tiled=True
        ).astype(jnp.float32),
        lax.psum_scatter(
            grad_dt.astype(jnp.bfloat16), "mb", scatter_dimension=0, tiled=True
        ).astype(jnp.float32),
        lax.psum_scatter(
            grad_out.astype(jnp.bfloat16), "mb", scatter_dimension=0, tiled=True
        ).astype(jnp.float32),
    )
    return (
        layer_out[None],
        in_grad[None],
        reduced[0].astype(jnp.bfloat16),
        reduced[1].astype(jnp.bfloat16),
        reduced[2].astype(jnp.bfloat16),
        reduced[3].astype(jnp.bfloat16),
    )


def solution(mesh):
    return jax.shard_map(
        per_device,
        mesh=mesh,
        in_specs=(
            P("mb", "head", None, None),
            P("mb"),
            P("mb", None),
            P(None, None, "head"),
            P("head", None),
            P("head", None),
            P(None, "head"),
            P(None, "head"),
            P("head"),
            P("head"),
            P("head"),
            P("head"),
            P("head", None),
            P("mb", "head", None),
        ),
        out_specs=(
            P("mb", "head", None),
            P("mb", "head", None),
            P("mb", None, "head"),
            P("mb", "head"),
            P("mb", "head"),
            P("mb", "head"),
        ),
        check_vma=False,
    )
```

profile of v0, /device:TPU:1, one launch (start us, length us, event | category | flops | bytes accessed | tf_op | source)
XLA Modules:
  0.0 2048.4 jit_solution(14737493015869717418)
XLA Ops:
  8.0 1.1 select_bitcast_fusion
  9.2 0.6 copy.104
  10.0 0.2 reduce-window.8
  10.1 0.1 convert_reduce_fusion
  10.2 0.1 slice_compare_fusion.1
  10.5 0.1 fusion.50
  10.6 0.1 concatenate.32
  10.7 0.1 concatenate.34
  10.9 0.1 pad_add_fusion
  11.0 786.1 %all-reduce.25.cloned.1.call-done = bf16[128,4096]{1,0:T(8,128)(2,1)} async-done(((bf16[128,4096]{1,0:T(8,128)(2,1)}), bf16[128,4096]{1,0:T(8,128)(2,1)}) %all-reduce.25.cloned.1.call-update) | async-done | bytes 1048592 | tf_op jit(solution)/shard_map/psum | solution.py:16
  797.1 2.5 fusion.3
  799.7 1.0 compare_select_fusion.2
  800.6 0.1 copy.100
  800.8 0.2 reduce_window_sum.29
  801.0 0.8 fusion.49
  801.8 0.1 copy.97
  801.9 0.4 fusion.88
  802.4 0.7 multiply_convert_fusion.1
  803.1 118.3 %all_gather.6 = bf16[128,2048]{0,1:T(8,128)(2,1)S(1)} all-gather(bf16[128,32]{0,1:T(8,128)(2,1)S(1)} %get-tuple-element.49), channel_id=1, replica_groups=mesh['head'=64,'mb'=4] {'head'}, dimensions={1}, use_global_device_ids=true | all-gather | bytes 532480 | tf_op jit(solution)/shard_map/all_gather | solution.py:111
  921.4 0.1 copy.98
  921.6 0.1 copy.99
  921.7 0.4 fusion.45
  922.1 0.4 fusion.9
  922.5 0.1 copy.103
  922.7 3.0 multiply_reduce_fusion.1
  925.8 202.5 %all-reduce.20 = (f32[128,8]{0,1:T(8,128)S(1)}, f32[128,8]{0,1:T(8,128)S(1)}) all-reduce(f32[128,8]{0,1:T(8,128)S(1)} %get-tuple-element.70, f32[128,8]{0,1:T(8,128)S(1)} %get-tuple-element.69), channel_id=1, replica_groups=mesh['head'=64,'mb'=4] {'head'}, use_global_device_ids=true, to_apply=%region_9.10 | all-reduce | flops 2048 | bytes 16384 | tf_op jit(solution)/shard_map/psum | solution.py:72
  1128.3 0.1 multiply_reduce_fusion.3
  1128.4 0.1 fusion.22
  1128.5 0.1 copy.107
  1128.6 1.1 fusion.70
  1129.7 1.0 multiply_reduce_fusion
  1130.6 0.1 copy.113
  1130.8 1.1 reduce_window_sum.30
  1132.0 0.3 convolution_convert_fusion.3
  1132.3 1.4 copy.123
  1133.9 1.4 fusion.8
  1135.2 1.4 fusion.7
  1136.6 0.9 copy-done.2
  1137.7 4.0 fusion
  1141.9 0.6 dynamic-slice.4
  1142.5 0.6 dynamic-slice
  1144.5 0.1 copy.108
  1144.6 0.1 fusion.25
  1144.7 0.1 fusion.26
  1144.8 0.1 fusion.27
  1144.9 2.1 convolution_convert_fusion
  1147.0 6.2 copy.115
  1153.2 3.8 fusion.1
  1157.1 0.2 reduce-scatter.9.cloned.1.call-start
  1157.3 0.4 copy-done.19
  1157.7 1.9 fusion.85
  1159.6 0.8 reduce-scatter.13.cloned.1.call-done
  1160.4 1.7 copy.124
  1162.1 403.5 %reduce-scatter.7.cloned.1.call-done = f32[128,32]{0,1:T(8,128)} async-done(((f32[128,2048]{0,1:T(8,128)}), f32[128,32]{0,1:T(8,128)}) %reduce-scatter.7.cloned.1.call-update) | async-done | bytes 16400 | tf_op jit(solution)/shard_map/reduce_scatter | solution.py:156
  1565.6 0.7 fusion.62
  1566.5 0.1 fusion.67
  1566.6 0.1 add_convert_fusion.1
  1566.7 2.1 convolution_add_fusion.1
  1568.8 1.9 convolution_add_fusion
  1570.8 1.0 convolution_convert_fusion.2
  1571.8 465.1 %all-reduce.28 = (bf16[128,4096]{1,0:T(8,128)(2,1)S(1)}, bf16[128,4096]{1,0:T(8,128)(2,1)S(1)}) all-reduce(f32[128,4096]{1,0:T(8,128)} %fusion.85, f32[128,4096]{1,0:T(8,128)} %convolution_add_fusion), channel_id=3, replica_groups=mesh['head'=64,'mb'=4] {'head'}, use_global_device_ids=true, to_apply=%region_7.8.clone | all-reduce | flops 1048576 | bytes 6291456
  2036.9 1.8 copy.116
  2038.7 2.2 constant_dynamic-slice_fusion
  2040.9 0.6 fusion.63
  (158 shorter events, 1.5 us)
Async XLA Ops:
  7.2 915.5 %copy-start = (bf16[128,4096]{1,0:T(8,128)(2,1)S(1)}, bf16[128,4096]{1,0:T(8,128)(2,1)}, u32[]{:S(2)}) copy-start(bf16[128,4096]{1,0:T(8,128)(2,1)} %param.26) | copy-start | bytes 3145732
  7.2 2.0 copy-start.11
  7.2 2.8 copy-start.51
  7.2 3.4 copy-start.52
  7.2 3.6 copy-start.43
  7.2 3.6 copy-start.44
  7.2 789.9 %all-reduce.25.cloned.1.call-start = ((), (), s32[]{:S(2)}) async-start(), calls=%async_computation.4 | async-start | bytes 2097152 | tf_op jit(solution)/shard_map/psum | solution.py:16
  9.1 913.5 %all-gather.3.cloned.1.call-start = ((), (), s32[]{:S(2)}) async-start(), calls=%async_computation.8 | async-start | bytes 2129920 | tf_op jit(solution)/shard_map/all_gather | solution.py:141
  9.9 789.8 %copy-start.9 = (bf16[2,4096]{1,0:T(2,128)(2,1)S(1)}, bf16[2,4096]{1,0:T(2,128)(2,1)}, u32[]{:S(2)}) copy-start(bf16[2,4096]{1,0:T(2,128)(2,1)} %param.19) | copy-start | bytes 49156
  9.9 789.8 %copy-start.53 = (f32[2]{0:T(128)S(1)}, f32[2]{0:T(128)}, u32[]{:S(2)}) copy-start(f32[2]{0:T(128)} %param.22) | copy-start | bytes 28
  9.9 1150.5 %reduce-scatter.13.cloned.1.call-start = ((), (), s32[]{:S(2)}) async-start(), calls=%async_computation.9 | async-start | bytes 1310720
  10.3 790.3 %copy-start.58 = (pred[126]{0:T(512)(128)(4,1)}, pred[126]{0:T(512)(128)(4,1)S(1)}, u32[]{:S(2)}) copy-start(pred[126]{0:T(512)(128)(4,1)S(1)} %slice_compare_fusion.1) | copy-start | bytes 382
  10.4 790.2 %copy-start.56 = (pred[125]{0:T(512)(128)(4,1)}, pred[125]{0:T(512)(128)(4,1)S(1)}, u32[]{:S(2)}) copy-start(pred[125]{0:T(512)(128)(4,1)S(1)} %slice_compare_fusion) | copy-start | bytes 379
  10.6 790.0 %copy-start.38 = (f32[2]{0:T(128)}, f32[2]{0:T(128)S(1)}, u32[]{:S(2)}) copy-start(f32[2]{0:T(128)S(1)} %exponential_negate_fusion) | copy-start | bytes 28
  10.8 790.2 %copy-start.28 = (f32[128]{0:T(128)}, f32[128]{0:T(128)S(1)}, u32[]{:S(2)}) copy-start(f32[128]{0:T(128)S(1)} %get-tuple-element.57) | copy-start | bytes 1540
  10.8 790.2 %copy-start.30 = (f32[128]{0:T(128)}, f32[128]{0:T(128)S(1)}, u32[]{:S(2)}) copy-start(f32[128]{0:T(128)S(1)} %get-tuple-element.59) | copy-start | bytes 1540
  10.8 790.2 %copy-start.32 = (f32[128]{0:T(128)}, f32[128]{0:T(128)S(1)}, u32[]{:S(2)}) copy-start(f32[128]{0:T(128)S(1)} %get-tuple-element.60) | copy-start | bytes 1540
  10.8 790.2 %copy-start.34 = (f32[128]{0:T(128)}, f32[128]{0:T(128)S(1)}, u32[]{:S(2)}) copy-start(f32[128]{0:T(128)S(1)} %get-tuple-element.58) | copy-start | bytes 1540
  10.8 791.5 %copy-start.20 = (f32[32]{0:T(128)}, f32[32]{0:T(128)S(1)}, u32[]{:S(2)}) copy-start(f32[32]{0:T(128)S(1)} %get-tuple-element.61) | copy-start | bytes 388
  10.9 791.5 %copy-start.22 = (f32[32]{0:T(128)}, f32[32]{0:T(128)S(1)}, u32[]{:S(2)}) copy-start(f32[32]{0:T(128)S(1)} %get-tuple-element.63) | copy-start | bytes 388
  10.9 791.5 %copy-start.24 = (f32[32]{0:T(128)}, f32[32]{0:T(128)S(1)}, u32[]{:S(2)}) copy-start(f32[32]{0:T(128)S(1)} %get-tuple-element.64) | copy-start | bytes 388
  10.9 791.5 %copy-start.26 = (f32[32]{0:T(128)}, f32[32]{0:T(128)S(1)}, u32[]{:S(2)}) copy-start(f32[32]{0:T(128)S(1)} %get-tuple-element.62) | copy-start | bytes 388
  11.0 791.4 %copy-start.41 = (pred[128]{0:T(512)(128)(4,1)}, pred[128]{0:T(512)(128)(4,1)S(1)}, u32[]{:S(2)}) copy-start(pred[128]{0:T(512)(128)(4,1)S(1)} %pad_add_fusion) | copy-start | bytes 388
  797.1 2.5 copy-start.1
  797.1 4.8 copy-start.3
  799.7 122.4 %copy-start.49 = (f32[2]{0:T(128)S(1)}, f32[2]{0:T(128)}, u32[]{:S(2)}) copy-start(f32[2]{0:T(128)} %param.24) | copy-start | bytes 28
  800.6 122.0 %copy-start.47 = (f32[128,2]{0,1:T(2,128)}, f32[128,2]{0,1:T(2,128)S(1)}, u32[]{:S(2)}) copy-start(f32[128,2]{0,1:T(2,128)S(1)} %get-tuple-element.65) | copy-start | bytes 3076
  800.6 122.1 %copy-start.45 = (f32[128]{0:T(128)S(1)}, f32[128]{0:T(128)}, u32[]{:S(2)}) copy-start(f32[128]{0:T(128)} %param.25) | copy-start | bytes 1540
  801.0 121.6 %copy-start.16 = (f32[2,128]{1,0:T(2,128)}, f32[2,128]{1,0:T(2,128)S(1)}, u32[]{:S(2)}) copy-start(f32[2,128]{1,0:T(2,128)S(1)} %copy.101) | copy-start | bytes 3076
  921.5 208.1 %copy-start.7 = (f32[128,128]{1,0:T(8,128)}, f32[128,128]{1,0:T(8,128)S(1)}, u32[]{:S(2)}) copy-start(f32[128,128]{1,0:T(8,128)S(1)} %copy.98) | copy-start | bytes 196612
  921.6 208.0 %copy-start.6 = (f32[128,128]{1,0:T(8,128)}, f32[128,128]{1,0:T(8,128)S(1)}, u32[]{:S(2)}) copy-start(f32[128,128]{1,0:T(8,128)S(1)} %copy.99) | copy-start | bytes 196612
  922.1 207.6 %copy-start.50 = (f32[2]{0:T(128)S(1)}, f32[2]{0:T(128)}, u32[]{:S(2)}) copy-start(f32[2]{0:T(128)} %param.24) | copy-start | bytes 28
  922.6 209.3 %copy-start.36 = (f32[128,2]{0,1:T(2,128)S(1)}, f32[128,2]{0,1:T(2,128)}, u32[]{:S(2)}) copy-start(f32[128,2]{0,1:T(2,128)} %get-tuple-element.71) | copy-start | bytes 3076
  922.6 209.3 %copy-start.39 = (f32[2]{0:T(128)S(1)}, f32[2]{0:T(128)}, u32[]{:S(2)}) copy-start(f32[2]{0:T(128)} %copy-done.38) | copy-start | bytes 28
  922.7 205.9 %copy-start.17 = (f32[2,128]{1,0:T(2,128)S(1)}, f32[2,128]{1,0:T(2,128)}, u32[]{:S(2)}) copy-start(f32[2,128]{1,0:T(2,128)} %copy-done.16) | copy-start | bytes 3076
  922.7 205.9 %copy-start.48 = (f32[128,2]{0,1:T(2,128)S(1)}, f32[128,2]{0,1:T(2,128)}, u32[]{:S(2)}) copy-start(f32[128,2]{0,1:T(2,128)} %copy-done.47) | copy-start | bytes 3076
  1128.4 5.3 copy-start.18
  1130.6 3.1 copy-start.12
  1131.9 1.8 copy-start.14
  1133.7 431.9 %reduce-scatter.7.cloned.1.call-start = ((), (), s32[]{:S(2)}) async-start(), calls=%async_computation.5 | async-start | bytes 1064960 | tf_op jit(solution)/shard_map/reduce_scatter | solution.py:156
  1136.6 5.2 copy-start.42
  1136.6 5.3 copy-start.55
  1136.6 5.9 copy-start.54
  1136.6 8.0 copy-start.35
  1137.6 6.8 copy-start.59
  1137.6 6.8 copy-start.57
  1137.6 6.8 copy-start.5
  1137.6 6.9 copy-start.4
  1137.6 7.1 copy-start.33
  1137.6 7.2 copy-start.31
  1137.7 7.3 copy-start.29
  1137.7 899.3 %reduce-scatter.11.cloned.1.call-start = ((), (), s32[]{:S(2)}) async-start(), calls=%async_computation.7 | async-start | bytes 1310720 | tf_op jit(solution)/shard_map/reduce_scatter | solution.py:184
  1141.8 897.0 %all-reduce.27.cloned.1.call-start = ((), (), s32[]{:S(2)}) async-start(), calls=%async_computation.10 | async-start | bytes 4194304
  1157.1 408.5 %copy-start.8 = (f32[128,32]{0,1:T(8,128)S(1)}, f32[128,32]{0,1:T(8,128)}, u32[]{:S(2)}) copy-start(f32[128,32]{0,1:T(8,128)} %get-tuple-element.50) | copy-start | bytes 49156
  1157.1 409.3 %copy-start.27 = (f32[32]{0:T(128)S(1)}, f32[32]{0:T(128)}, u32[]{:S(2)}) copy-start(f32[32]{0:T(128)} %copy-done.26) | copy-start | bytes 388
  1157.1 409.3 %copy-start.25 = (f32[32]{0:T(128)S(1)}, f32[32]{0:T(128)}, u32[]{:S(2)}) copy-start(f32[32]{0:T(128)} %copy-done.24) | copy-start | bytes 388
  1157.1 409.4 %copy-start.23 = (f32[32]{0:T(128)S(1)}, f32[32]{0:T(128)}, u32[]{:S(2)}) copy-start(f32[32]{0:T(128)} %copy-done.22) | copy-start | bytes 388
  1157.1 409.5 %copy-start.21 = (f32[32]{0:T(128)S(1)}, f32[32]{0:T(128)}, u32[]{:S(2)}) copy-start(f32[32]{0:T(128)} %copy-done.20) | copy-start | bytes 388
  1157.1 884.5 %reduce-scatter.9.cloned.1.call-start = ((), (), s32[]{:S(2)}) async-start(), calls=%async_computation.6 | async-start | bytes 327680 | tf_op jit(solution)/shard_map/reduce_scatter | solution.py:178
  1566.7 2.1 copy-start.10
  1566.7 2.1 copy-start.13
  1566.7 2.1 copy-start.15
  1566.7 2.1 copy-start.37
  1566.7 2.1 copy-start.40
  (3 other events, 2.3 us)
Sparse Core Ops, SparseCore 0:
  10.7 786.3 all-reduce.24
  801.8 84.0 all-gather.2
  1133.8 26.5 reduce-scatter.12
  1162.7 402.8 reduce-scatter.6
  1568.2 35.9 reduce-scatter.10
  1606.7 108.5 all-reduce.26
  1718.5 24.1 reduce-scatter.8
where the time goes:
time: 2080 us; the launch traced here: 2050 us
  waiting for transfers between devices  1190 us (57%)
  blocking collectives  786 us (38%)
  matrix products  29.5 us (1%)
    psum x1, waiting for transfers between devices, spread_2(): return lax.psum(kept, axis)  786 us
    unnamed x1, blocking collectives  465 us
    reduce_scatter x1, waiting for transfers between devices, per_device(): lax.psum_scatter(d_state_all, 'head', scatter_dimension=1, tiled=True)  404 us
    psum x1, blocking collectives, group_total(): totals = lax.psum(partial_value[:, None] * group_mask[None, :], 'head')  202 us
    all_gather x1, blocking collectives, per_device(): lax.all_gather(state_act.astype(jnp.bfloat16), 'head', axis=1, tiled=True)  118 us
  transfers between devices with their start and end apart: 7, of which 3 were waited for; matrix products, arithmetic and copies ran while one was open for 2% of the time, Pallas kernels for 0%

commit v1 on v0

v1 whole, which is shorter than its diff:
```python
import jax
import jax.numpy as jnp
from jax import lax
from jax.experimental import pallas as pl
from jax.experimental.pallas import tpu as pltpu
from jax.sharding import PartitionSpec as P

T = 128
EPS = 1e-05
WIDTH = 1024
HI = lax.Precision.HIGHEST
MESH = pl.DeviceIdType.MESH
BF = jnp.bfloat16
F32 = jnp.float32


def sigmoid(v):
    return 1.0 / (1.0 + jnp.exp(-v))


def hdot(a, b, dims):
    return lax.dot_general(a, b, (dims, ((), ())), precision=HI, preferred_element_type=F32)


def bdot(a, b, dims):
    return lax.dot_general(a, b, (dims, ((), ())), preferred_element_type=F32)


NN = ((1,), (0,))
NT = ((1,), (1,))
TN = ((0,), (0,))


class Ids:
    def __init__(self):
        self.used = 0

    def take(self, count):
        first = self.used
        self.used += count
        return first


def staged(last):
    return dict(
        p=pltpu.VMEM((4, 4, 2, 2, 4, 16, 128), BF),
        r1=pltpu.VMEM((4, 4, 2, 4, 16, 128), BF),
        q=pltpu.VMEM((4, 4, 2, 4, 16, 128), BF),
        r2x=pltpu.VMEM((3, 2, 4, 2, 16, 128), BF),
        r2y=pltpu.VMEM((3, 2, 2, 4, 16, 128), BF),
        qx=pltpu.VMEM((2, 4, 2, 16, 128), BF),
        qy=pltpu.VMEM((2, 2, 4, 16, 128), BF),
        r3x=pltpu.VMEM((3, 2, 2, 16, 128), BF),
        r3y=pltpu.VMEM((3, 2, 2, 16, 128), BF),
        t=pltpu.VMEM((4, 2, 16, 128), BF),
        r4=pltpu.VMEM(last, BF),
    )


def rows_trade():
    return dict(
        v=pltpu.VMEM((64, 128), F32), g=pltpu.VMEM((64, 128), F32), r=pltpu.VMEM((64, 128), F32)
    )


N_SEM = 240

SCRATCH = dict(
    arr=pltpu.VMEM((T, 4096), BF),
    win=pltpu.VMEM((8192, 128), BF),
    wf=pltpu.VMEM((2, 512, 128), F32),
    wxz=pltpu.VMEM((4096, 256), BF),
    w2=pltpu.VMEM((128, 4096), BF),
    wdtf=pltpu.VMEM((16, 4096), F32),
    wout=pltpu.VMEM((128, 4096), BF),
    cbc=pltpu.VMEM((8, 128), F32),
    ax=pltpu.VMEM((7, 4, 2, 2, 4, 16, 128), BF),
    ao=pltpu.VMEM((7, 4, 2, 2, 4, 16, 128), BF),
    x=pltpu.VMEM((T, 4096), BF),
    o=pltpu.VMEM((T, 4096), BF),
    ss=pltpu.VMEM((32, 128), BF),
    bc=pltpu.VMEM((8, 32, 128), BF),
    norm=pltpu.VMEM((8, 8, 128), F32),
    dbcs=pltpu.VMEM((8, 32, 128), F32),
    dbcr=pltpu.VMEM((8, 32, 128), F32),
    dx=pltpu.VMEM((4, 128, 128), BF),
    dz=pltpu.VMEM((4, 128, 128), BF),
    nm=pltpu.VMEM((4, 128, 128), BF),
    d2=pltpu.VMEM((4, 48, 128), BF),
    gf=pltpu.VMEM((2, 256, 128), F32),
    sx=staged((4, 2, 16, 128)),
    slo=staged((4, 16, 128)),
    sig=staged((4, 16, 128)),
    tog=rows_trade(),
    tlo=rows_trade(),
    tig=rows_trade(),
    ssem=pltpu.SemaphoreType.DMA((N_SEM,)),
    rsem=pltpu.SemaphoreType.DMA((N_SEM,)),
    lsem=pltpu.SemaphoreType.DMA((8,)),
)


def mixer_kernel(
    own_ref, doc_ref, dtb_ref, alog_ref, skip_ref, cx_ref, cbc_ref, gain_ref, wdt_ref, og_ref,
    arr_hbm, win_hbm, wbc_hbm, wout_hbm,
    lo_out, ig_out, gin_out, gbc_out, gdt_out, go_out,
    s,
):
    h = lax.axis_index("head")
    m = lax.axis_index("mb")
    zh = h // 32
    x = (h // 8) % 4
    y = (h // 2) % 4
    c = h % 2
    j = h % 8
    g = h // 8
    g_t = (h % 32) // 4
    part = zh * 4 + h % 4
    ssem, rsem, lsem = s["ssem"], s["rsem"], s["lsem"]
    ids = Ids()
    sent = []

    def head_of(zh_, x_, y_, c_):
        return zh_ * 32 + x_ * 8 + y_ * 2 + c_

    def copy(src, dst, i, head, mb, r=None):
        return pltpu.make_async_remote_copy(
            src_ref=src, dst_ref=dst, send_sem=ssem.at[i], recv_sem=rsem.at[i if r is None else r],
            device_id=(head, mb), device_id_type=MESH,
        )

    def start(cp):
        cp.start()
        sent.append(cp)
        return cp

    loc = [
        pltpu.make_async_copy(arr_hbm, s["arr"], lsem.at[0]),
        pltpu.make_async_copy(win_hbm, s["win"], lsem.at[1]),
        pltpu.make_async_copy(wbc_hbm, s["w2"].at[0:32], lsem.at[2]),
        pltpu.make_async_copy(wout_hbm, s["wout"], lsem.at[3]),
    ]
    for cp in loc:
        cp.start()

    barrier = pltpu.get_barrier_semaphore()
    count = 0
    peers = [(head_of(zh, x, y, 1 - c), m), (head_of(1 - zh, x, y, c), m)]
    for d in range(1, 4):
        peers.append((head_of(zh, (x + d) % 4, y, c), m))
        peers.append((h, (m + d) % 4))
    for d in range(1, 8):
        peers.append((8 * g + (j + d) % 8, m))
    for head, mb in peers:
        pl.semaphore_signal(barrier, inc=1, device_id=(head, mb), device_id_type=MESH)
        count += 1
    own_parts = [4 * g + k for k in range(4)] + [32 + 4 * g + k for k in range(4)]
    targets = [8 * g_t + k for k in range(8)]
    for head in own_parts + targets:
        pl.semaphore_signal(barrier, inc=1, device_id=(head, m), device_id_type=MESH)
        count += 1

    s["cbc"][...] = jnp.zeros((8, 128), F32)
    s["cbc"][0:4, 0:32] = cbc_ref[...]
    s["wdtf"][...] = jnp.zeros((16, 4096), F32)
    s["wdtf"][0:2, :] = wdt_ref[...].astype(F32)
    s["w2"][32:48, :] = s["wdtf"][...].astype(BF)
    s["w2"][48:128, :] = jnp.zeros((80, 4096), BF)

    sx = s["sx"]
    loc[0].wait()

    def split_arr(i, _):
        v = s["arr"][:, pl.ds(pl.multiple_of(i * 256, 256), 256)]
        for cc in range(2):
            sx["p"][i // 4, i % 4, cc] = v[:, cc * 128:(cc + 1) * 128].reshape(2, 4, 16, 128)
        return 0

    lax.fori_loop(0, 16, split_arr, 0)
    pl.semaphore_wait(barrier, count)

    owner = own_ref[0]
    o_zh, o_x, o_y, o_c = owner // 32, (owner // 8) % 4, (owner // 2) % 4, owner % 2

    def combine(own, received, picks):
        if picks is None:
            total = own.astype(F32)
            for v in received:
                total = total + v.astype(F32)
            return total
        value = own
        for v, pick in zip(received, picks):
            value = lax.select(pick, v, value)
        return value

    def stage1_copy(b, i):
        return copy(b["p"].at[:, :, 1 - c], b["r1"], i, head_of(zh, x, y, 1 - c), m)

    def stage1_merge(b, picks):
        def one(q, _):
            b["q"][q] = combine(b["p"][q, :, c], [b["r1"][q]], picks and picks["c"]).astype(BF)
            return 0
        lax.fori_loop(0, 4, one, 0)

    def stage2_copies(b, i):
        cps = []
        for d in range(1, 4):
            x2, y2 = (x + d) % 4, (y + d) % 4
            cps.append(copy(b["q"].at[0:2, :, :, x2], b["r2x"].at[d - 1], i + 2 * d - 2, head_of(zh, x2, y, c), m))
            cps.append(copy(b["q"].at[2:4, y2], b["r2y"].at[d - 1], i + 2 * d - 1, head_of(zh, x, y2, c), m))
        return cps

    def stage2_merge(b, picks):
        for q in range(2):
            b["qx"][q] = combine(b["q"][q, :, :, x], [b["r2x"][d, q] for d in range(3)], picks and picks["x"]).astype(BF)
            b["qy"][q] = combine(b["q"][2 + q, y], [b["r2y"][d, q] for d in range(3)], picks and picks["y"]).astype(BF)

    def stage3_copies(b, i):
        cps = []
        for d in range(1, 4):
            x2, y2 = (x + d) % 4, (y + d) % 4
            cps.append(copy(b["qx"].at[:, y2], b["r3x"].at[d - 1], i + 2 * d - 2, head_of(zh, x, y2, c), m))
            cps.append(copy(b["qy"].at[:, :, x2], b["r3y"].at[d - 1], i + 2 * d - 1, head_of(zh, x2, y, c), m))
        return cps

    def stage3_merge(b, picks):
        b["t"][0:2] = combine(b["qx"][:, y], [b["r3x"][d] for d in range(3)], picks and picks["y"]).astype(BF)
        b["t"][2:4] = combine(b["qy"][:, :, x], [b["r3y"][d] for d in range(3)], picks and picks["x"]).astype(BF)

    other_zh = head_of(1 - zh, x, y, c)

    def gather1(a, s1, s2, i):
        cps = []
        for d in range(1, 4):
            x2, y2 = (x + d) % 4, (y + d) % 4
            r1, r2 = a.at[s1, y, c, :, x], a.at[s2, y, c, :, x]
            cps.append(copy(r1, r1, i + 2 * d - 2, head_of(zh, x, y2, c), m))
            cps.append(copy(r2, r2, i + 2 * d - 1, head_of(zh, x2, y, c), m))
        return cps

    def gather2(a, s1, s2, i):
        cps = []
        for d in range(1, 4):
            x2, y2 = (x + d) % 4, (y + d) % 4
            r1, r2 = a.at[s1, :, c, :, x], a.at[s2, y, c]
            cps.append(copy(r1, r1, i + 2 * d - 2, head_of(zh, x2, y, c), m))
            cps.append(copy(r2, r2, i + 2 * d - 1, head_of(zh, x, y2, c), m))
        return cps

    def gather3(a, part_of, i):
        ref = a.at[part_of, :, c]
        return [copy(ref, ref, i, head_of(zh, x, y, 1 - c), m)]

    def go(cps):
        for cp in cps:
            start(cp)
        return cps

    def got(cps):
        for cp in cps:
            cp.wait_recv()

    def trade(b, i):
        cps = []
        for d in range(1, 8):
            k = (j + d) % 8
            src = b["g"].at[pl.ds(pl.multiple_of(k * 8, 8), 8)]
            dst = b["r"].at[pl.ds(pl.multiple_of(j * 8, 8), 8)]
            cps.append(copy(src, dst, i + d - 1, 8 * g + k, m))
        mine = pl.ds(pl.multiple_of(j * 8, 8), 8)
        b["r"][mine, :] = b["g"][mine, :]
        return cps

    lane = lax.broadcasted_iota(jnp.int32, (T, 128), 1)
    row = lax.broadcasted_iota(jnp.int32, (T, 128), 0)

    def unpack_weights(first, last):
        def one(i, _):
            k = i % 2
            s["wf"][k] = s["win"][pl.ds(pl.multiple_of(i * 512, 512), 512), :].astype(F32)
            at = pl.ds(pl.multiple_of(i * 256, 256), 256)
            s["wxz"][at, 0:128] = s["wf"][k, pl.ds(0, 256, stride=2), :].astype(BF)
            s["wxz"][at, 128:256] = s["wf"][k, pl.ds(1, 256, stride=2), :].astype(BF)
            return 0
        lax.fori_loop(first, last, one, 0)

    picks = dict(
        c=[o_c != c],
        x=[o_x == (x + 4 - d) % 4 for d in range(1, 4)],
        y=[o_y == (y + 4 - d) % 4 for d in range(1, 4)],
    )
    a_x, a_o = s["ax"], s["ao"]
    x1 = go([stage1_copy(sx, ids.take(1))])
    tog = s["tog"]
    og = og_ref[...].astype(F32)
    for k in range(8):
        for q in range(4):
            tog["g"][k * 8 + q * 2:k * 8 + q * 2 + 2, :] = og[:, q * 1024 + k * 128:q * 1024 + k * 128 + 128]
    o1 = go(trade(tog, ids.take(7)))
    got(x1)
    stage1_merge(sx, picks)
    x2 = go(stage2_copies(sx, ids.take(6)))
    got(o1)
    for q in range(4):
        for tt in range(2):
            tog["v"][pl.ds(q * 16 + tt, 8, stride=2), :] = tog["r"][pl.ds(q * 2 + tt, 8, stride=8), :]
    a_o[0:4, y, c, zh, x] = tog["v"][...].reshape(4, 16, 128).astype(BF)
    cps = []
    i0 = ids.take(3)
    for d in range(1, 4):
        m2 = (m + d) % 4
        cps.append(copy(a_o.at[m2, y, c, zh, x], a_o.at[7 - d, y, c, zh, x], i0 + d - 1, h, m2))
    oc = go(cps)
    oz_ref = a_o.at[0:4, y, c, zh, x]
    oz = go([copy(oz_ref, oz_ref, ids.take(1), other_zh, m)])
    loc[1].wait()
    unpack_weights(0, 3)
    got(x2)
    stage2_merge(sx, picks)
    x3 = go(stage3_copies(sx, ids.take(6)))
    got(oz)
    q01, q23 = slice(0, 2), slice(2, 4)
    og1 = go(gather1(a_o, q01, q23, ids.take(6)))
    unpack_weights(3, 6)
    got(x3)
    stage3_merge(sx, picks)
    x4 = go([copy(sx["t"], sx["r4"], ids.take(1), other_zh, m)])
    got(oc)
    ocz_ref = a_o.at[4:7, y, c, zh, x]
    ocz = go([copy(ocz_ref, ocz_ref, ids.take(1), other_zh, m)])
    got(og1)
    unpack_weights(6, 9)
    got(x4)
    a_x[0:4, y, c, :, x] = combine(sx["t"][...], [sx["r4"][...]], [o_zh != zh])
    xg1 = go(gather1(a_x, q01, q23, ids.take(6)))
    i0 = ids.take(3)
    cps = []
    for d in range(1, 4):
        m2 = (m + d) % 4
        cps.append(copy(a_x.at[m2, y, c, :, x], a_x.at[7 - d, y, c, :, x], i0 + d - 1, h, m2))
    xc = go(cps)
    og2 = go(gather2(a_o, q01, q23, ids.take(6)))
    unpack_weights(9, 12)
    got(xg1)
    xg2 = go(gather2(a_x, q01, q23, ids.take(6)))
    unpack_weights(12, 16)
    got(og2)
    got(xg2)
    xg3 = go(gather3(a_x, slice(0, 4), ids.take(1)))
    og3 = go(gather3(a_o, slice(0, 4), ids.take(1)))

    def assemble(a, dst, cc):
        def one(i, _):
            at = pl.ds(pl.multiple_of(i * 256 + cc * 128, 128), 128)
            dst[:, at] = a[i // 4, i % 4, cc].reshape(128, 128)
            return 0
        lax.fori_loop(0, 16, one, 0)

    assemble(a_x, s["x"], c)
    loc[2].wait()
    got(xg3)
    assemble(a_x, s["x"], 1 - c)

    e1 = doc_ref[0, 0]
    e2 = e1 + doc_ref[0, 1]
    e3 = e2 + doc_ref[0, 2]
    e4 = e3 + doc_ref[0, 3]

    def doc_of(t):
        return sum((t >= e).astype(jnp.int32) for e in (e1, e2, e3, e4))

    doc_row = doc_of(row)
    same = [None] + [(row >= o) & (doc_of(row - o) == doc_row) for o in range(1, 4)]
    visible = (row >= lane) & (doc_row == doc_of(lane))

    def conv(v, taps):
        result = v * taps[3:4]
        for o in range(1, 4):
            result = result + jnp.where(same[o], pltpu.roll(v, o, 0), 0.0) * taps[3 - o:4 - o]
        return result

    def conv_back(d, taps):
        result = d * taps[3:4]
        for o in range(1, 4):
            result = result + pltpu.roll(jnp.where(same[o], d, 0.0), T - o, 0) * taps[3 - o:4 - o]
        return result

    p2 = bdot(s["x"][...], s["w2"][...], NT)
    taps_bc = s["cbc"][...]
    bc_pre = conv(p2, taps_bc)
    bc_sig = sigmoid(bc_pre)
    s["ss"][...] = jnp.transpose(bc_pre * bc_sig)[0:32].astype(BF)
    i_bc = ids.take(8)
    for k in range(8):
        head = 8 * g_t + k

        @pl.when(head != h)
        def _():
            copy(s["ss"], s["bc"].at[part], i_bc + k, head, m, i_bc + part).start()

        @pl.when(head == h)
        def _():
            pltpu.make_async_copy(s["ss"], s["bc"].at[part], rsem.at[i_bc + part]).start()

    pxz = bdot(s["x"][...], s["wxz"][...], NN)
    z = pxz[:, 128:256]
    taps_x = cx_ref[...]
    x_pre = conv(pxz[:, 0:128], taps_x)
    x_sig = sigmoid(x_pre)
    x_conv = x_pre * x_sig
    z_sig = sigmoid(z)
    z_silu = z * z_sig
    low = lane < 64
    tri = jnp.where(row >= lane, 1.0, 0.0)
    raws, rates, steps = [], [], []
    for e in range(2):
        raw = jnp.broadcast_to(p2[:, 32 + e:33 + e], (T, 128)) + dtb_ref[e]
        raws.append(raw)
        rates.append(-jnp.exp(jnp.full((T, 128), alog_ref[e], F32)))
        steps.append(jnp.maximum(raw, 0.0) + jnp.log1p(jnp.exp(-jnp.abs(raw))))
    step = jnp.where(low, steps[0], steps[1])
    cum = hdot(tri, jnp.where(low, steps[0] * rates[0], steps[1] * rates[1]), NN)
    decays = []
    for e in range(2):
        col = jnp.broadcast_to(cum[:, 64 * e:64 * e + 1], (T, 128))
        gap = col - jnp.transpose(col)
        decays.append(jnp.where(visible, jnp.exp(jnp.where(visible, gap, 0.0)), 0.0))
    scaled = x_conv * step
    skip = jnp.where(low, skip_ref[0], skip_ref[1])

    assemble(a_o, s["o"], c)
    got(og3)
    assemble(a_o, s["o"], 1 - c)
    loc[3].wait()
    weighted = bdot(s["o"][...], s["wout"][...], NT) * gain_ref[...]

    got(xc)
    k1, k2 = slice(4, 5), slice(5, 7)
    cxg1 = go(gather1(a_x, k1, k2, ids.take(6)))
    got(ocz)
    l1, l2 = slice(4, 6), slice(6, 7)
    cog1 = go(gather1(a_o, l1, l2, ids.take(6)))

    for k in range(8):
        copy(s["ss"], s["bc"].at[k], i_bc + k, other_zh, m).wait_recv()
    b_t = s["bc"][0:4].reshape(128, 128)
    c_t = s["bc"][4:8].reshape(128, 128)
    scores = bdot(c_t, b_t, TN)
    mixes = [scores * decays[0], scores * decays[1]]
    zero = jnp.zeros((T, 128), F32)
    scaled2 = jnp.concatenate([jnp.where(low, scaled, zero), jnp.where(low, zero, scaled)], axis=0)
    state = hdot(jnp.concatenate(mixes, axis=1), scaled2, NN) + skip * x_conv
    gated = state * z_silu
    squares = jnp.sum(gated * gated, axis=1, keepdims=True)
    inners = jnp.sum(weighted * gated, axis=1, keepdims=True)
    nmat = jnp.where(lane == 0, squares, jnp.where(lane == 1, inners, 0.0))
    s["norm"][j] = jnp.transpose(nmat)[0:8]
    i_n = ids.take(7)
    ncp = []
    for d in range(1, 8):
        ncp.append(copy(s["norm"].at[j], s["norm"].at[j], i_n + d - 1, 8 * g + (j + d) % 8, m))
    go(ncp)
    got(cxg1)
    cxg2 = go(gather2(a_x, k1, k2, ids.take(6)))
    got(cog1)
    cog2 = go(gather2(a_o, l1, l2, ids.take(6)))
    got(ncp)
    total = jnp.sum(s["norm"][...], axis=0)
    tcol = jnp.transpose(jnp.concatenate([total, jnp.zeros((120, 128), F32)], axis=0))
    inverse = jnp.broadcast_to(lax.rsqrt(tcol[:, 0:1] * (1.0 / WIDTH) + EPS), (T, 128))
    inner = jnp.broadcast_to(tcol[:, 1:2] * (1.0 / WIDTH), (T, 128))
    normed = (gated * inverse * gain_ref[...]).astype(BF)
    s["nm"][0] = normed
    d_gated = inverse * weighted - gated * (inverse * inverse * inverse * inner)

    d_state = d_gated * z_silu
    d_z = d_gated * state * (z_sig * (1.0 + z * (1.0 - z_sig)))
    s["dz"][0] = d_z.astype(BF)
    dy0, dy1 = jnp.where(low, d_state, zero), jnp.where(low, zero, d_state)
    d_mix = [hdot(dy0, scaled, NT), hdot(dy1, scaled, NT)]
    d_scores = d_mix[0] * decays[0] + d_mix[1] * decays[1]
    s["dbcs"][0:4] = hdot(c_t.astype(F32), d_scores, NN).reshape(4, 32, 128)
    s["dbcs"][4:8] = hdot(b_t.astype(F32), d_scores, NT).reshape(4, 32, 128)
    i_d = ids.take(8)
    for k in range(8):
        head = own_parts[k]

        @pl.when(head != h)
        def _():
            copy(s["dbcs"].at[k], s["dbcr"].at[j], i_d + k, head, m, i_d + j).start()

        @pl.when(head == h)
        def _():
            pltpu.make_async_copy(s["dbcs"].at[k], s["dbcr"].at[j], rsem.at[i_d + j]).start()

    def to_mb(ref, i):
        cps = []
        for d in range(1, 4):
            cps.append(copy(ref.at[0], ref.at[4 - d], i + d - 1, h, (m + d) % 4))
        return go(cps)

    n_mb = to_mb(s["nm"], ids.take(3))
    z_mb = to_mb(s["dz"], ids.take(3))

    slo, sig = s["slo"], s["sig"]

    def lo_half(cc):
        def one(i, _):
            at = pl.ds(pl.multiple_of(i * 256 + cc * 128, 128), 128)
            v = bdot(normed, s["wout"][:, at], NN)
            slo["p"][i // 4, i % 4, cc] = v.astype(BF).reshape(2, 4, 16, 128)
            return 0
        lax.fori_loop(0, 16, one, 0)

    lo_half(1 - c)
    lo1 = go([stage1_copy(slo, ids.take(1))])
    lo_half(c)

    d_scaled = hdot(
        jnp.concatenate(mixes, axis=0), jnp.concatenate([dy0, dy1], axis=0), TN
    )
    d_xconv = skip * d_state + d_scaled * step
    d_x = conv_back(d_xconv * (x_sig * (1.0 + x_pre * (1.0 - x_sig))), taps_x)
    s["dx"][0] = d_x.astype(BF)
    x_mb = to_mb(s["dx"], ids.take(3))
    through = d_scaled * x_conv
    d_raws = []
    for e in range(2):
        mine = low if e == 0 else lane >= 64
        gap_grad = d_mix[e] * mixes[e]
        d_cum = jnp.sum(gap_grad - jnp.transpose(gap_grad), axis=1, keepdims=True)
        back = hdot(tri, jnp.broadcast_to(d_cum, (T, 128)), TN)
        d_step = jnp.sum(jnp.where(mine, through, 0.0), axis=1, keepdims=True) + rates[e] * back
        d_raws.append(d_step * sigmoid(raws[e]))

    got(cxg2)
    cxg3 = go(gather3(a_x, slice(4, 7), ids.take(1)))
    got(cog2)
    cog3 = go(gather3(a_o, slice(4, 7), ids.take(1)))

    for k in range(8):
        copy(s["dbcs"].at[k], s["dbcr"].at[k], i_d + k, other_zh, m).wait_recv()
    d_act = jnp.transpose(
        jnp.concatenate([jnp.sum(s["dbcr"][...], axis=0), jnp.zeros((96, 128), F32)], axis=0)
    )
    d_bc = conv_back(d_act * (bc_sig * (1.0 + bc_pre * (1.0 - bc_sig))), taps_bc)
    d2 = jnp.where(lane == 32, d_raws[0], jnp.where(lane == 33, d_raws[1], d_bc))
    d2_b = d2.astype(BF)
    s["d2"][0] = jnp.transpose(d2)[0:48].astype(BF)
    d2_mb = to_mb(s["d2"], ids.take(3))

    d_proj = jnp.concatenate([s["dx"][0], s["dz"][0]], axis=1)

    def ig_half(cc):
        def one(i, _):
            at = pl.ds(pl.multiple_of(i * 256 + cc * 128, 128), 128)
            v = bdot(d_proj, s["wxz"][at, :], NT) + bdot(d2_b, s["w2"][:, at], NN)
            sig["p"][i // 4, i % 4, cc] = v.astype(BF).reshape(2, 4, 16, 128)
            return 0
        lax.fori_loop(0, 16, one, 0)

    ig_half(1 - c)
    ig1 = go([stage1_copy(sig, ids.take(1))])
    ig_half(c)
    got(lo1)
    stage1_merge(slo, None)
    got(ig1)
    stage1_merge(sig, None)
    ig2 = go(stage2_copies(sig, ids.take(6)))
    lo2 = go(stage2_copies(slo, ids.take(6)))

    got(n_mb)
    got(cog3)
    nm_all = s["nm"][...].reshape(512, 128)

    def grad_out(i, _):
        yy, cc = i // 2, i % 2
        lhs = jnp.concatenate(
            [a_o[m, yy, cc].reshape(128, 128)] + [a_o[k, yy, cc].reshape(128, 128) for k in range(4, 7)], axis=0
        )
        go_out[pl.ds(pl.multiple_of(i * 128, 128), 128), :] = bdot(lhs, nm_all, TN).astype(BF)
        return 0

    lax.fori_loop(0, 8, grad_out, 0)

    def stage4(b, i):
        return go([copy(b["t"].at[:, 1 - zh], b["r4"], i, other_zh, m)])

    def stage5(b, t, i):
        t["v"][...] = (b["t"][:, zh].astype(F32) + b["r4"][...].astype(F32)).reshape(64, 128)
        for q in range(4):
            for tt in range(2):
                t["g"][pl.ds(q * 2 + tt, 8, stride=8), :] = t["v"][pl.ds(q * 16 + tt, 8, stride=2), :]
        return go(trade(t, i))

    def finish(t, out):
        for k in range(8):
            for q in range(4):
                at = q * 1024 + k * 128
                out[:, at:at + 128] = t["r"][k * 8 + q * 2:k * 8 + q * 2 + 2, :].astype(BF)

    got(ig2)
    stage2_merge(sig, None)
    ig3 = go(stage3_copies(sig, ids.take(6)))
    got(lo2)
    stage2_merge(slo, None)
    lo3 = go(stage3_copies(slo, ids.take(6)))
    got(x_mb)
    got(z_mb)
    got(d2_mb)
    got(cxg3)
    d_all = jnp.concatenate(
        [s["dx"][...].reshape(512, 128), s["dz"][...].reshape(512, 128)], axis=1
    )
    d2_all = jnp.concatenate([s["d2"][k] for k in range(4)], axis=1)

    def grad_in(i, _):
        yy, cc, k = i // 2, i % 2, i % 2
        lhs = jnp.concatenate(
            [a_x[m, yy, cc].reshape(128, 128)] + [a_x[k_, yy, cc].reshape(128, 128) for k_ in range(4, 7)], axis=0
        )
        r = bdot(lhs, d_all, TN)
        s["gf"][k, pl.ds(0, 128, stride=2), :] = r[:, 0:128]
        s["gf"][k, pl.ds(1, 128, stride=2), :] = r[:, 128:256]
        gin_out[pl.ds(pl.multiple_of(i * 256, 256), 256), :] = s["gf"][k].astype(BF)
        small = bdot(d2_all, lhs, NN)
        at = pl.ds(pl.multiple_of(i * 128, 128), 128)
        gbc_out[:, at] = small[0:32].astype(BF)
        gdt_out[:, at] = small[32:34].astype(BF)
        return 0

    lax.fori_loop(0, 4, grad_in, 0)
    got(ig3)
    stage3_merge(sig, None)
    ig4 = stage4(sig, ids.take(1))
    got(lo3)
    stage3_merge(slo, None)
    lo4 = stage4(slo, ids.take(1))
    lax.fori_loop(4, 8, grad_in, 0)
    got(ig4)
    ig5 = stage5(sig, s["tig"], ids.take(7))
    got(lo4)
    lo5 = stage5(slo, s["tlo"], ids.take(7))
    got(ig5)
    finish(s["tig"], ig_out)
    got(lo5)
    finish(s["tlo"], lo_out)

    for cp in sent:
        cp.wait_send()
    for k in range(8):
        @pl.when(8 * g_t + k != h)
        def _():
            copy(s["ss"], s["bc"].at[part], i_bc + k, 8 * g_t + k, m).wait_send()

        @pl.when(own_parts[k] != h)
        def _():
            copy(s["dbcs"].at[k], s["dbcr"].at[j], i_d + k, own_parts[k], m).wait_send()

    assert ids.used <= N_SEM


def per_device(
    arrivals, owners, doc_lengths, w_in, w_bc, w_dt, conv_x, conv_bc, dt_bias, a_log, skip_scale,
    norm_gain, w_out, out_grad,
):
    smem = pl.BlockSpec(memory_space=pltpu.SMEM)
    vmem = pl.BlockSpec(memory_space=pltpu.VMEM)
    hbm = pl.BlockSpec(memory_space=pl.ANY)
    sds = jax.ShapeDtypeStruct
    lo, ig, gin, gbc, gdt, gout = pl.pallas_call(
        mixer_kernel,
        out_shape=(
            sds((2, 4096), BF), sds((2, 4096), BF), sds((2048, 128), BF), sds((32, 1024), BF),
            sds((2, 1024), BF), sds((1024, 128), BF),
        ),
        in_specs=[smem] * 5 + [vmem] * 5 + [hbm] * 4,
        out_specs=(vmem,) * 6,
        scratch_shapes=[SCRATCH],
        compiler_params=pltpu.CompilerParams(
            collective_id=0, has_side_effects=True, vmem_limit_bytes=56 * 1024 * 1024
        ),
    )(
        owners, doc_lengths, dt_bias, a_log, skip_scale, conv_x, conv_bc,
        norm_gain.reshape(1, 128), w_dt, out_grad.reshape(2, 4096),
        arrivals.reshape(T, 4096), w_in.reshape(8192, 128), w_bc, w_out,
    )
    return (
        lo[None], ig[None], gin.reshape(1024, 2, 128), gbc.T, gdt.T, gout,
    )


def solution(mesh):
    return jax.shard_map(
        per_device,
        mesh=mesh,
        in_specs=(
            P("mb", "head", None, None),
            P("mb"),
            P("mb", None),
            P(None, None, "head"),
            P("head", None),
            P("head", None),
            P(None, "head"),
            P(None, "head"),
            P("head"),
            P("head"),
            P("head"),
            P("head"),
            P("head", None),
            P("mb", "head", None),
        ),
        out_specs=(
            P("mb", "head", None),
            P("mb", "head", None),
            P("mb", None, "head"),
            P("mb", "head"),
            P("mb", "head"),
            P("mb", "head"),
        ),
        check_vma=False,
    )
```

time: 2080 us -> 105 us (0.05); the launches traced: 2050 us -> 104 us
  waiting for transfers between devices: 1190 us -> 0 us
  blocking collectives: 786 us -> 0 us
  Pallas kernels: 0 us -> 93.8 us
  matrix products: 29.5 us -> 0 us
    psum x1 -> x0, waiting for transfers between devices: 786 us -> none  [spread_2(): return lax.psum(kept, axis)]
    unnamed x1 -> x0, blocking collectives: 465 us -> none
    reduce_scatter x3 -> x0, waiting for transfers between devices: 404 us -> none  [the longest x1 404 us: per_device(): lax.psum_scatter(d_state_all, 'head', scatter_dimension=1, tiled=True)]
    psum x1 -> x0, blocking collectives: 202 us -> none  [group_total(): totals = lax.psum(partial_value[:, None] * group_mask[None, :], 'head')]
    all_gather x1 -> x0, blocking collectives: 118 us -> none  [per_device(): lax.all_gather(state_act.astype(jnp.bfloat16), 'head', axis=1, tiled=True)]
    pallas_call x0 -> x1, Pallas kernels: none -> 93.8 us  [per_device(): pl.pallas_call(mixer_kernel, out_shape=(sds((2, 4096), BF), sds((2, 4096)...]
    dot_general x18 -> x0, matrix products: 29.5 us -> none  [the longest x1 4.04 us: per_device(): lax.dot_general(shard_rows, normed, columns, preferred_element_type=jnp.f...]
  transfers between devices with their start and end apart: 7 -> 0, of which waited for: 3 -> 0; matrix products, arithmetic and copies ran while one was open for 2% -> 0% of each run, Pallas kernels for 0% -> 0%
where the time goes in v1:
time: 105 us; the launch traced here: 104 us
  Pallas kernels  93.8 us (89%)
  local copies, waits for them, and re-layouts  9.27 us (9%)
  between operations  1.29 us (1%)
    pallas_call x1, Pallas kernels, per_device(): pl.pallas_call(mixer_kernel, out_shape=(sds((2, 4096), BF), sds((2, 4096)...  93.8 us
    unnamed x6, local copies, waits for them, and re-layouts  9.27 us

profile of v1, /device:TPU:1, one launch (start us, length us, event | category | flops | bytes accessed | tf_op | source)
XLA Modules:
  0.0 104.4 jit_solution(3178439717767312755)
XLA Ops:
  1.3 93.8 %shard_map.181 = (bf16[2,4096]{1,0:T(2,128)(2,1)}, bf16[2,4096]{1,0:T(2,128)(2,1)}, bf16[2048,128]{1,0:T(8,128)(2,1)}, bf16[32,1024]{1,0:T(8,128)(2,1)}, bf16[2,...) custom-call(s32[1]{0:T(128)S(6)} %copy.26.own_ref, s32[1,4]{1,0:T(1,128)} %doc_ref.1, f32[2]{0:T(128)} %dtb_ref.1, f32[2]{0:T(128)} %alog_ref.1, ...), custom_call_target="tpu_custom_call" | custom-call | tf_op jit(solution)/shard_map/pallas_call | solution.py:671
  95.1 1.3 %copy.27 = bf16[1,2,4096]{2,1,0:T(2,128)(2,1)} copy(bf16[1,2,4096]{2,1,0:T(2,128)(2,1)} %bitcast.15) | data formatting | bytes 32768
  96.4 1.3 %copy.28 = bf16[1,2,4096]{2,1,0:T(2,128)(2,1)} copy(bf16[1,2,4096]{2,1,0:T(2,128)(2,1)} %bitcast.14) | data formatting | bytes 32768
  97.8 2.2 %copy.29 = bf16[1024,2,128]{2,1,0:T(2,128)(2,1)} copy(bf16[1024,2,128]{2,1,0:T(2,128)(2,1)} %bitcast.11) | data formatting | bytes 1048576
  100.0 1.5 %copy.30 = bf16[1024,32]{0,1:T(8,128)(2,1)} copy(bf16[1024,32]{0,1:T(8,128)(2,1)} %bitcast.12) | data formatting | bytes 131072
  101.4 1.3 %copy.31 = bf16[1024,2]{0,1:T(2,128)(2,1)} copy(bf16[1024,2]{0,1:T(2,128)(2,1)} %bitcast.16) | data formatting | bytes 8192
  102.7 1.7 %copy.32 = bf16[1024,128]{1,0:T(8,128)(2,1)} copy(bf16[1024,128]{1,0:T(8,128)(2,1)} %get-tuple-element.29) | data formatting | bytes 524288

commit v2 on v1

--- a/solution.py
+++ b/solution.py
@@ -63,7 +63,8 @@
     )
 
 
-N_SEM = 240
+N_RECV = 52
+N_SEND = 66
 
 SCRATCH = dict(
     arr=pltpu.VMEM((T, 4096), BF),
@@ -94,8 +95,8 @@
     tog=rows_trade(),
     tlo=rows_trade(),
     tig=rows_trade(),
-    ssem=pltpu.SemaphoreType.DMA((N_SEM,)),
-    rsem=pltpu.SemaphoreType.DMA((N_SEM,)),
+    ssem=pltpu.SemaphoreType.DMA((N_SEND,)),
+    rsem=pltpu.SemaphoreType.DMA((N_RECV,)),
     lsem=pltpu.SemaphoreType.DMA((8,)),
 )
 
@@ -117,22 +118,34 @@
     g_t = (h % 32) // 4
     part = zh * 4 + h % 4
     ssem, rsem, lsem = s["ssem"], s["rsem"], s["lsem"]
-    ids = Ids()
+    rids, sids = Ids(), Ids()
     sent = []
 
     def head_of(zh_, x_, y_, c_):
         return zh_ * 32 + x_ * 8 + y_ * 2 + c_
 
-    def copy(src, dst, i, head, mb, r=None):
+    def copy(src, dst, i, r, head, mb):
         return pltpu.make_async_remote_copy(
-            src_ref=src, dst_ref=dst, send_sem=ssem.at[i], recv_sem=rsem.at[i if r is None else r],
+            src_ref=src, dst_ref=dst, send_sem=ssem.at[i], recv_sem=rsem.at[r],
             device_id=(head, mb), device_id_type=MESH,
         )
 
-    def start(cp):
-        cp.start()
-        sent.append(cp)
-        return cp
+    def wait_all(ref, sem):
+        pltpu.make_async_copy(ref, ref, sem).wait()
+
+    def go(groups):
+        waits = []
+        for copies, whole in groups:
+            i, r = sids.take(1), rids.take(1)
+            for src, dst, head, mb in copies:
+                copy(src, dst, i, r, head, mb).start()
+            waits.append((whole, r))
+            sent.append((whole, i))
+        return waits
+
+    def got(waits):
+        for whole, r in waits:
+            wait_all(whole, rsem.at[r])
 
     loc = [
         pltpu.make_async_copy(arr_hbm, s["arr"], lsem.at[0]),
@@ -176,7 +189,7 @@
             sx["p"][i // 4, i % 4, cc] = v[:, cc * 128:(cc + 1) * 128].reshape(2, 4, 16, 128)
         return 0
 
-    lax.fori_loop(0, 16, split_arr, 0)
+    lax.fori_loop(0, 16, split_arr, 0, unroll=4)
     pl.semaphore_wait(barrier, count)
 
     owner = own_ref[0]
@@ -193,8 +206,8 @@
             value = lax.select(pick, v, value)
         return value
 
-    def stage1_copy(b, i):
-        return copy(b["p"].at[:, :, 1 - c], b["r1"], i, head_of(zh, x, y, 1 - c), m)
+    def stage1_copies(b):
+        return [([(b["p"].at[:, :, 1 - c], b["r1"], head_of(zh, x, y, 1 - c), m)], b["r1"])]
 
     def stage1_merge(b, picks):
         def one(q, _):
@@ -202,26 +215,26 @@
             return 0
         lax.fori_loop(0, 4, one, 0)
 
-    def stage2_copies(b, i):
-        cps = []
+    def stage2_copies(b):
+        along_x, along_y = [], []
         for d in range(1, 4):
             x2, y2 = (x + d) % 4, (y + d) % 4
-            cps.append(copy(b["q"].at[0:2, :, :, x2], b["r2x"].at[d - 1], i + 2 * d - 2, head_of(zh, x2, y, c), m))
-            cps.append(copy(b["q"].at[2:4, y2], b["r2y"].at[d - 1], i + 2 * d - 1, head_of(zh, x, y2, c), m))
-        return cps
+            along_x.append((b["q"].at[0:2, :, :, x2], b["r2x"].at[d - 1], head_of(zh, x2, y, c), m))
+            along_y.append((b["q"].at[2:4, y2], b["r2y"].at[d - 1], head_of(zh, x, y2, c), m))
+        return [(along_x, b["r2x"]), (along_y, b["r2y"])]
 
     def stage2_merge(b, picks):
         for q in range(2):
             b["qx"][q] = combine(b["q"][q, :, :, x], [b["r2x"][d, q] for d in range(3)], picks and picks["x"]).astype(BF)
             b["qy"][q] = combine(b["q"][2 + q, y], [b["r2y"][d, q] for d in range(3)], picks and picks["y"]).astype(BF)
 
-    def stage3_copies(b, i):
-        cps = []
+    def stage3_copies(b):
+        along_x, along_y = [], []
         for d in range(1, 4):
             x2, y2 = (x + d) % 4, (y + d) % 4
-            cps.append(copy(b["qx"].at[:, y2], b["r3x"].at[d - 1], i + 2 * d - 2, head_of(zh, x, y2, c), m))
-            cps.append(copy(b["qy"].at[:, :, x2], b["r3y"].at[d - 1], i + 2 * d - 1, head_of(zh, x2, y, c), m))
-        return cps
+            along_y.append((b["qx"].at[:, y2], b["r3x"].at[d - 1], head_of(zh, x, y2, c), m))
+            along_x.append((b["qy"].at[:, :, x2], b["r3y"].at[d - 1], head_of(zh, x2, y, c), m))
+        return [(along_y, b["r3x"]), (along_x, b["r3y"])]
 
     def stage3_merge(b, picks):
         b["t"][0:2] = combine(b["qx"][:, y], [b["r3x"][d] for d in range(3)], picks and picks["y"]).astype(BF)
@@ -229,47 +242,38 @@
 
     other_zh = head_of(1 - zh, x, y, c)
 
-    def gather1(a, s1, s2, i):
-        cps = []
+    def gather1(a, s1, s2):
+        along_x, along_y = [], []
+        r1, r2 = a.at[s1, y, c, :, x], a.at[s2, y, c, :, x]
         for d in range(1, 4):
             x2, y2 = (x + d) % 4, (y + d) % 4
-            r1, r2 = a.at[s1, y, c, :, x], a.at[s2, y, c, :, x]
-            cps.append(copy(r1, r1, i + 2 * d - 2, head_of(zh, x, y2, c), m))
-            cps.append(copy(r2, r2, i + 2 * d - 1, head_of(zh, x2, y, c), m))
-        return cps
-
-    def gather2(a, s1, s2, i):
-        cps = []
+            along_y.append((r1, r1, head_of(zh, x, y2, c), m))
+            along_x.append((r2, r2, head_of(zh, x2, y, c), m))
+        return [(along_y, a.at[s1, 0:3, c, :, x]), (along_x, a.at[s2, y, c, :, 0:3])]
+
+    def gather2(a, s1, s2):
+        along_x, along_y = [], []
+        r1, r2 = a.at[s1, :, c, :, x], a.at[s2, y, c]
         for d in range(1, 4):
             x2, y2 = (x + d) % 4, (y + d) % 4
-            r1, r2 = a.at[s1, :, c, :, x], a.at[s2, y, c]
-            cps.append(copy(r1, r1, i + 2 * d - 2, head_of(zh, x2, y, c), m))
-            cps.append(copy(r2, r2, i + 2 * d - 1, head_of(zh, x, y2, c), m))
-        return cps
-
-    def gather3(a, part_of, i):
+            along_x.append((r1, r1, head_of(zh, x2, y, c), m))
+            along_y.append((r2, r2, head_of(zh, x, y2, c), m))
+        return [(along_x, a.at[s1, :, c, :, 0:3]), (along_y, a.at[s2, 0:3, c])]
+
+    def gather3(a, part_of):
         ref = a.at[part_of, :, c]
-        return [copy(ref, ref, i, head_of(zh, x, y, 1 - c), m)]
-
-    def go(cps):
-        for cp in cps:
-            start(cp)
-        return cps
-
-    def got(cps):
-        for cp in cps:
-            cp.wait_recv()
-
-    def trade(b, i):
+        return [([(ref, ref, head_of(zh, x, y, 1 - c), m)], ref)]
+
+    def trade(b):
         cps = []
         for d in range(1, 8):
             k = (j + d) % 8
             src = b["g"].at[pl.ds(pl.multiple_of(k * 8, 8), 8)]
             dst = b["r"].at[pl.ds(pl.multiple_of(j * 8, 8), 8)]
-            cps.append(copy(src, dst, i + d - 1, 8 * g + k, m))
+            cps.append((src, dst, 8 * g + k, m))
         mine = pl.ds(pl.multiple_of(j * 8, 8), 8)
         b["r"][mine, :] = b["g"][mine, :]
-        return cps
+        return [(cps, b["r"].at[0:56])]
 
     lane = lax.broadcasted_iota(jnp.int32, (T, 128), 1)
     row = lax.broadcasted_iota(jnp.int32, (T, 128), 0)
@@ -290,71 +294,73 @@
         y=[o_y == (y + 4 - d) % 4 for d in range(1, 4)],
     )
     a_x, a_o = s["ax"], s["ao"]
-    x1 = go([stage1_copy(sx, ids.take(1))])
+    x1 = go(stage1_copies(sx))
     tog = s["tog"]
     og = og_ref[...].astype(F32)
     for k in range(8):
         for q in range(4):
             tog["g"][k * 8 + q * 2:k * 8 + q * 2 + 2, :] = og[:, q * 1024 + k * 128:q * 1024 + k * 128 + 128]
-    o1 = go(trade(tog, ids.take(7)))
+    o1 = go(trade(tog))
     got(x1)
     stage1_merge(sx, picks)
-    x2 = go(stage2_copies(sx, ids.take(6)))
+    x2 = go(stage2_copies(sx))
     got(o1)
     for q in range(4):
         for tt in range(2):
             tog["v"][pl.ds(q * 16 + tt, 8, stride=2), :] = tog["r"][pl.ds(q * 2 + tt, 8, stride=8), :]
     a_o[0:4, y, c, zh, x] = tog["v"][...].reshape(4, 16, 128).astype(BF)
     cps = []
-    i0 = ids.take(3)
     for d in range(1, 4):
         m2 = (m + d) % 4
-        cps.append(copy(a_o.at[m2, y, c, zh, x], a_o.at[7 - d, y, c, zh, x], i0 + d - 1, h, m2))
-    oc = go(cps)
+        cps.append((a_o.at[m2, y, c, zh, x], a_o.at[7 - d, y, c, zh, x], h, m2))
+    oc = go([(cps, a_o.at[4:7, y, c, zh, x])])
     oz_ref = a_o.at[0:4, y, c, zh, x]
-    oz = go([copy(oz_ref, oz_ref, ids.take(1), other_zh, m)])
+    oz = go([([(oz_ref, oz_ref, other_zh, m)], oz_ref)])
     loc[1].wait()
     unpack_weights(0, 3)
     got(x2)
     stage2_merge(sx, picks)
-    x3 = go(stage3_copies(sx, ids.take(6)))
+    x3 = go(stage3_copies(sx))
     got(oz)
     q01, q23 = slice(0, 2), slice(2, 4)
-    og1 = go(gather1(a_o, q01, q23, ids.take(6)))
+    og1 = go(gather1(a_o, q01, q23))
     unpack_weights(3, 6)
     got(x3)
     stage3_merge(sx, picks)
-    x4 = go([copy(sx["t"], sx["r4"], ids.take(1), other_zh, m)])
+    x4 = go([([(sx["t"], sx["r4"], other_zh, m)], sx["r4"])])
     got(oc)
     ocz_ref = a_o.at[4:7, y, c, zh, x]
-    ocz = go([copy(ocz_ref, ocz_ref, ids.take(1), other_zh, m)])
+    ocz = go([([(ocz_ref, ocz_ref, other_zh, m)], ocz_ref)])
     got(og1)
     unpack_weights(6, 9)
     got(x4)
     a_x[0:4, y, c, :, x] = combine(sx["t"][...], [sx["r4"][...]], [o_zh != zh])
-    xg1 = go(gather1(a_x, q01, q23, ids.take(6)))
-    i0 = ids.take(3)
+    xg1 = go(gather1(a_x, q01, q23))
     cps = []
     for d in range(1, 4):
         m2 = (m + d) % 4
-        cps.append(copy(a_x.at[m2, y, c, :, x], a_x.at[7 - d, y, c, :, x], i0 + d - 1, h, m2))
-    xc = go(cps)
-    og2 = go(gather2(a_o, q01, q23, ids.take(6)))
+        cps.append((a_x.at[m2, y, c, :, x], a_x.at[7 - d, y, c, :, x], h, m2))
+    xc = go([(cps, a_x.at[4:7, y, c, :, x])])
+    k1, k2 = slice(4, 5), slice(5, 7)
+    l1, l2 = slice(4, 6), slice(6, 7)
     unpack_weights(9, 12)
     got(xg1)
-    xg2 = go(gather2(a_x, q01, q23, ids.take(6)))
+    xg2 = go(gather2(a_x, q01, q23))
+    got(ocz)
+    cog1 = go(gather1(a_o, l1, l2))
+    got(xc)
+    cxg1 = go(gather1(a_x, k1, k2))
     unpack_weights(12, 16)
-    got(og2)
     got(xg2)
-    xg3 = go(gather3(a_x, slice(0, 4), ids.take(1)))
-    og3 = go(gather3(a_o, slice(0, 4), ids.take(1)))
+    xg3 = go(gather3(a_x, slice(0, 4)))
+    og2 = go(gather2(a_o, q01, q23))
 
     def assemble(a, dst, cc):
         def one(i, _):
             at = pl.ds(pl.multiple_of(i * 256 + cc * 128, 128), 128)
             dst[:, at] = a[i // 4, i % 4, cc].reshape(128, 128)
             return 0
-        lax.fori_loop(0, 16, one, 0)
+        lax.fori_loop(0, 16, one, 0, unroll=8)
 
     assemble(a_x, s["x"], c)
     loc[2].wait()
@@ -390,19 +396,26 @@
     bc_pre = conv(p2, taps_bc)
     bc_sig = sigmoid(bc_pre)
     s["ss"][...] = jnp.transpose(bc_pre * bc_sig)[0:32].astype(BF)
-    i_bc = ids.take(8)
+    i_bc, r_bc = sids.take(8), rids.take(1)
     for k in range(8):
         head = 8 * g_t + k
 
         @pl.when(head != h)
         def _():
-            copy(s["ss"], s["bc"].at[part], i_bc + k, head, m, i_bc + part).start()
+            copy(s["ss"], s["bc"].at[part], i_bc + k, r_bc, head, m).start()
 
         @pl.when(head == h)
         def _():
-            pltpu.make_async_copy(s["ss"], s["bc"].at[part], rsem.at[i_bc + part]).start()
+            pltpu.make_async_copy(s["ss"], s["bc"].at[part], rsem.at[r_bc]).start()
+
+    got(cxg1)
+    cxg2 = go(gather2(a_x, k1, k2))
+    got(cog1)
+    cog2 = go(gather2(a_o, l1, l2))
 
     pxz = bdot(s["x"][...], s["wxz"][...], NN)
+    got(og2)
+    og3 = go(gather3(a_o, slice(0, 4)))
     z = pxz[:, 128:256]
     taps_x = cx_ref[...]
     x_pre = conv(pxz[:, 0:128], taps_x)
@@ -434,15 +447,7 @@
     loc[3].wait()
     weighted = bdot(s["o"][...], s["wout"][...], NT) * gain_ref[...]
 
-    got(xc)
-    k1, k2 = slice(4, 5), slice(5, 7)
-    cxg1 = go(gather1(a_x, k1, k2, ids.take(6)))
-    got(ocz)
-    l1, l2 = slice(4, 6), slice(6, 7)
-    cog1 = go(gather1(a_o, l1, l2, ids.take(6)))
-
-    for k in range(8):
-        copy(s["ss"], s["bc"].at[k], i_bc + k, other_zh, m).wait_recv()
+    wait_all(s["bc"], rsem.at[r_bc])
     b_t = s["bc"][0:4].reshape(128, 128)
     c_t = s["bc"][4:8].reshape(128, 128)
     scores = bdot(c_t, b_t, TN)
@@ -455,15 +460,12 @@
     inners = jnp.sum(weighted * gated, axis=1, keepdims=True)
     nmat = jnp.where(lane == 0, squares, jnp.where(lane == 1, inners, 0.0))
     s["norm"][j] = jnp.transpose(nmat)[0:8]
-    i_n = ids.take(7)
-    ncp = []
-    for d in range(1, 8):
-        ncp.append(copy(s["norm"].at[j], s["norm"].at[j], i_n + d - 1, 8 * g + (j + d) % 8, m))
-    go(ncp)
-    got(cxg1)
-    cxg2 = go(gather2(a_x, k1, k2, ids.take(6)))
-    got(cog1)
-    cog2 = go(gather2(a_o, l1, l2, ids.take(6)))
+    cps = [(s["norm"].at[j], s["norm"].at[j], 8 * g + (j + d) % 8, m) for d in range(1, 8)]
+    ncp = go([(cps, s["norm"].at[0:7])])
+    got(cxg2)
+    cxg3 = go(gather3(a_x, slice(4, 7)))
+    got(cog2)
+    cog3 = go(gather3(a_o, slice(4, 7)))
     got(ncp)
     total = jnp.sum(s["norm"][...], axis=0)
     tcol = jnp.transpose(jnp.concatenate([total, jnp.zeros((120, 128), F32)], axis=0))
@@ -481,26 +483,24 @@
     d_scores = d_mix[0] * decays[0] + d_mix[1] * decays[1]
     s["dbcs"][0:4] = hdot(c_t.astype(F32), d_scores, NN).reshape(4, 32, 128)
     s["dbcs"][4:8] = hdot(b_t.astype(F32), d_scores, NT).reshape(4, 32, 128)
-    i_d = ids.take(8)
+    i_d, r_d = sids.take(8), rids.take(1)
     for k in range(8):
         head = own_parts[k]
 
         @pl.when(head != h)
         def _():
-            copy(s["dbcs"].at[k], s["dbcr"].at[j], i_d + k, head, m, i_d + j).start()
+            copy(s["dbcs"].at[k], s["dbcr"].at[j], i_d + k, r_d, head, m).start()
 
         @pl.when(head == h)
         def _():
-            pltpu.make_async_copy(s["dbcs"].at[k], s["dbcr"].at[j], rsem.at[i_d + j]).start()
-
-    def to_mb(ref, i):
-        cps = []
-        for d in range(1, 4):
-            cps.append(copy(ref.at[0], ref.at[4 - d], i + d - 1, h, (m + d) % 4))
-        return go(cps)
-
-    n_mb = to_mb(s["nm"], ids.take(3))
-    z_mb = to_mb(s["dz"], ids.take(3))
+            pltpu.make_async_copy(s["dbcs"].at[k], s["dbcr"].at[j], rsem.at[r_d]).start()
+
+    def to_mb(ref):
+        cps = [(ref.at[0], ref.at[4 - d], h, (m + d) % 4) for d in range(1, 4)]
+        return go([(cps, ref.at[1:4])])
+
+    n_mb = to_mb(s["nm"])
+    z_mb = to_mb(s["dz"])
 
     slo, sig = s["slo"], s["sig"]
 
@@ -510,10 +510,10 @@
             v = bdot(normed, s["wout"][:, at], NN)
             slo["p"][i // 4, i % 4, cc] = v.astype(BF).reshape(2, 4, 16, 128)
             return 0
-        lax.fori_loop(0, 16, one, 0)
+        lax.fori_loop(0, 16, one, 0, unroll=8)
 
     lo_half(1 - c)
-    lo1 = go([stage1_copy(slo, ids.take(1))])
+    lo1 = go(stage1_copies(slo))
     lo_half(c)
 
     d_scaled = hdot(
@@ -522,7 +522,7 @@
     d_xconv = skip * d_state + d_scaled * step
     d_x = conv_back(d_xconv * (x_sig * (1.0 + x_pre * (1.0 - x_sig))), taps_x)
     s["dx"][0] = d_x.astype(BF)
-    x_mb = to_mb(s["dx"], ids.take(3))
+    x_mb = to_mb(s["dx"])
     through = d_scaled * x_conv
     d_raws = []
     for e in range(2):
@@ -533,13 +533,11 @@
         d_step = jnp.sum(jnp.where(mine, through, 0.0), axis=1, keepdims=True) + rates[e] * back
         d_raws.append(d_step * sigmoid(raws[e]))
 
-    got(cxg2)
-    cxg3 = go(gather3(a_x, slice(4, 7), ids.take(1)))
-    got(cog2)
-    cog3 = go(gather3(a_o, slice(4, 7), ids.take(1)))
-
-    for k in range(8):
-        copy(s["dbcs"].at[k], s["dbcr"].at[k], i_d + k, other_zh, m).wait_recv()
+    got(lo1)
+    stage1_merge(slo, None)
+    lo2 = go(stage2_copies(slo))
+
+    wait_all(s["dbcr"], rsem.at[r_d])
     d_act = jnp.transpose(
         jnp.concatenate([jnp.sum(s["dbcr"][...], axis=0), jnp.zeros((96, 128), F32)], axis=0)
     )
@@ -547,7 +545,7 @@
     d2 = jnp.where(lane == 32, d_raws[0], jnp.where(lane == 33, d_raws[1], d_bc))
     d2_b = d2.astype(BF)
     s["d2"][0] = jnp.transpose(d2)[0:48].astype(BF)
-    d2_mb = to_mb(s["d2"], ids.take(3))
+    d2_mb = to_mb(s["d2"])
 
     d_proj = jnp.concatenate([s["dx"][0], s["dz"][0]], axis=1)
 
@@ -557,17 +555,17 @@
             v = bdot(d_proj, s["wxz"][at, :], NT) + bdot(d2_b, s["w2"][:, at], NN)
             sig["p"][i // 4, i % 4, cc] = v.astype(BF).reshape(2, 4, 16, 128)
             return 0
-        lax.fori_loop(0, 16, one, 0)
+        lax.fori_loop(0, 16, one, 0, unroll=8)
 
     ig_half(1 - c)
-    ig1 = go([stage1_copy(sig, ids.take(1))])
+    ig1 = go(stage1_copies(sig))
     ig_half(c)
-    got(lo1)
-    stage1_merge(slo, None)
+    got(lo2)
+    stage2_merge(slo, None)
+    lo3 = go(stage3_copies(slo))
     got(ig1)
     stage1_merge(sig, None)
-    ig2 = go(stage2_copies(sig, ids.take(6)))
-    lo2 = go(stage2_copies(slo, ids.take(6)))
+    ig2 = go(stage2_copies(sig))
 
     got(n_mb)
     got(cog3)
@@ -581,17 +579,17 @@
         go_out[pl.ds(pl.multiple_of(i * 128, 128), 128), :] = bdot(lhs, nm_all, TN).astype(BF)
         return 0
 
-    lax.fori_loop(0, 8, grad_out, 0)
-
-    def stage4(b, i):
-        return go([copy(b["t"].at[:, 1 - zh], b["r4"], i, other_zh, m)])
-
-    def stage5(b, t, i):
+    lax.fori_loop(0, 8, grad_out, 0, unroll=4)
+
+    def stage4(b):
+        return go([([(b["t"].at[:, 1 - zh], b["r4"], other_zh, m)], b["r4"])])
+
+    def stage5(b, t):
         t["v"][...] = (b["t"][:, zh].astype(F32) + b["r4"][...].astype(F32)).reshape(64, 128)
         for q in range(4):
             for tt in range(2):
                 t["g"][pl.ds(q * 2 + tt, 8, stride=8), :] = t["v"][pl.ds(q * 16 + tt, 8, stride=2), :]
-        return go(trade(t, i))
+        return go(trade(t))
 
     def finish(t, out):
         for k in range(8):
@@ -599,12 +597,9 @@
                 at = q * 1024 + k * 128
                 out[:, at:at + 128] = t["r"][k * 8 + q * 2:k * 8 + q * 2 + 2, :].astype(BF)
 
-    got(ig2)
-    stage2_merge(sig, None)
-    ig3 = go(stage3_copies(sig, ids.take(6)))
-    got(lo2)
-    stage2_merge(slo, None)
-    lo3 = go(stage3_copies(slo, ids.take(6)))
+    got(lo3)
+    stage3_merge(slo, None)
+    lo4 = stage4(slo)
     got(x_mb)
     got(z_mb)
     got(d2_mb)
@@ -629,35 +624,41 @@
         gdt_out[:, at] = small[32:34].astype(BF)
         return 0
 
-    lax.fori_loop(0, 4, grad_in, 0)
+    lax.fori_loop(0, 3, grad_in, 0)
+    got(ig2)
+    stage2_merge(sig, None)
+    ig3 = go(stage3_copies(sig))
+    lax.fori_loop(3, 5, grad_in, 0)
+    got(lo4)
+    lo5 = stage5(slo, s["tlo"])
     got(ig3)
     stage3_merge(sig, None)
-    ig4 = stage4(sig, ids.take(1))
-    got(lo3)
-    stage3_merge(slo, None)
-    lo4 = stage4(slo, ids.take(1))
-    lax.fori_loop(4, 8, grad_in, 0)
+    ig4 = stage4(sig)
+    lax.fori_loop(5, 8, grad_in, 0)
+    got(lo5)
+    finish(s["tlo"], lo_out)
     got(ig4)
-    ig5 = stage5(sig, s["tig"], ids.take(7))
-    got(lo4)
-    lo5 = stage5(slo, s["tlo"], ids.take(7))
+    ig5 = stage5(sig, s["tig"])
     got(ig5)
     finish(s["tig"], ig_out)
-    got(lo5)
-    finish(s["tlo"], lo_out)
-
-    for cp in sent:
-        cp.wait_send()
+
+    for whole, i in sent:
+        wait_all(whole, ssem.at[i])
     for k in range(8):
         @pl.when(8 * g_t + k != h)
         def _():
-            copy(s["ss"], s["bc"].at[part], i_bc + k, 8 * g_t + k, m).wait_send()
+            wait_all(s["ss"], ssem.at[i_bc + k])
 
         @pl.when(own_parts[k] != h)
         def _():
-            copy(s["dbcs"].at[k], s["dbcr"].at[j], i_d + k, own_parts[k], m).wait_send()
-
-    assert ids.used <= N_SEM
+            wait_all(s["dbcs"].at[k], ssem.at[i_d + k])
+
+    assert rids.used <= N_RECV and sids.used <= N_SEND, (rids.used, sids.used)
+
+
+def place_kernel(*refs):
+    for source, result in zip(refs[:6], refs[6:]):
+        result[...] = source[...]
 
 
 def per_device(
@@ -668,12 +669,13 @@
     vmem = pl.BlockSpec(memory_space=pltpu.VMEM)
     hbm = pl.BlockSpec(memory_space=pl.ANY)
     sds = jax.ShapeDtypeStruct
-    lo, ig, gin, gbc, gdt, gout = pl.pallas_call(
+    shapes = (
+        sds((2, 4096), BF), sds((2, 4096), BF), sds((2048, 128), BF), sds((32, 1024), BF),
+        sds((2, 1024), BF), sds((1024, 128), BF),
+    )
+    made = pl.pallas_call(
         mixer_kernel,
-        out_shape=(
-            sds((2, 4096), BF), sds((2, 4096), BF), sds((2048, 128), BF), sds((32, 1024), BF),
-            sds((2, 1024), BF), sds((1024, 128), BF),
-        ),
+        out_shape=shapes,
         in_specs=[smem] * 5 + [vmem] * 5 + [hbm] * 4,
         out_specs=(vmem,) * 6,
         scratch_shapes=[SCRATCH],
@@ -685,6 +687,12 @@
         norm_gain.reshape(1, 128), w_dt, out_grad.reshape(2, 4096),
         arrivals.reshape(T, 4096), w_in.reshape(8192, 128), w_bc, w_out,
     )
+    lo, ig, gin, gbc, gdt, gout = pl.pallas_call(
+        place_kernel,
+        out_shape=shapes,
+        in_specs=[vmem] * 6,
+        out_specs=(vmem,) * 6,
+    )(*made)
     return (
         lo[None], ig[None], gin.reshape(1024, 2, 128), gbc.T, gdt.T, gout,
     )

time: 105 us -> 89.4 us (0.85)
  local copies, waits for them, and re-layouts: 9.27 us -> 0 us
  Pallas kernels: 93.8 us -> 86.8 us
    unnamed x6 -> x0, local copies, waits for them, and re-layouts: 9.27 us -> none
    pallas_call x1 -> x2, Pallas kernels: 93.8 us -> 86.8 us  [the longest x1 84.7 us: per_device(): pl.pallas_call(mixer_kernel, out_shape=shapes, in_specs=[smem] * 5 + [vme...]
where the time goes in v2:
time: 89.4 us; the launch traced here: 88.1 us
  Pallas kernels  86.8 us (97%)
  between operations  1.29 us (1%)
    pallas_call x1, Pallas kernels, per_device(): pl.pallas_call(mixer_kernel, out_shape=shapes, in_specs=[smem] * 5 + [vme...  84.7 us
    pallas_call x1, Pallas kernels, per_device(): pl.pallas_call(place_kernel, out_shape=shapes, in_specs=[vmem] * 6, out_s...  2.11 us

profile of v2, /device:TPU:1, one launch (start us, length us, event | category | flops | bytes accessed | tf_op | source)
XLA Modules:
  0.0 88.1 jit_solution(1997315868057610206)
XLA Ops:
  1.3 84.7 %shard_map.181 = (bf16[2,4096]{1,0:T(2,128)(2,1)}, bf16[2,4096]{1,0:T(2,128)(2,1)}, bf16[2048,128]{1,0:T(8,128)(2,1)}, bf16[32,1024]{1,0:T(8,128)(2,1)}, bf16[2,...) custom-call(s32[1]{0:T(128)S(6)} %copy.20.own_ref, s32[1,4]{1,0:T(1,128)} %doc_ref.1, f32[2]{0:T(128)} %dtb_ref.1, f32[2]{0:T(128)} %alog_ref.1, ...), custom_call_target="tpu_custom_call" | custom-call | tf_op jit(solution)/shard_map/pallas_call | solution.py:676
  86.0 2.1 %shard_map.182 = (bf16[2,4096]{1,0:T(2,128)(2,1)}, bf16[2,4096]{1,0:T(2,128)(2,1)}, bf16[2048,128]{1,0:T(8,128)(2,1)}, bf16[32,1024]{1,0:T(8,128)(2,1)}, bf16[2,...) custom-call(bf16[2,4096]{1,0:T(2,128)(2,1)} %get-tuple-element.18.refs_0_, bf16[2,4096]{1,0:T(2,128)(2,1)} %get-tuple-element.19.refs_1_, ...), custom_call_target="tpu_custom_call" | custom-call | tf_op jit(solution)/shard_map/pallas_call | solution.py:690

commit v3 on v2

--- a/solution.py
+++ b/solution.py
@@ -46,12 +46,12 @@
         p=pltpu.VMEM((4, 4, 2, 2, 4, 16, 128), BF),
         r1=pltpu.VMEM((4, 4, 2, 4, 16, 128), BF),
         q=pltpu.VMEM((4, 4, 2, 4, 16, 128), BF),
-        r2x=pltpu.VMEM((3, 2, 4, 2, 16, 128), BF),
-        r2y=pltpu.VMEM((3, 2, 2, 4, 16, 128), BF),
+        r2x=pltpu.VMEM((2, 3, 4, 2, 16, 128), BF),
+        r2y=pltpu.VMEM((2, 3, 2, 4, 16, 128), BF),
         qx=pltpu.VMEM((2, 4, 2, 16, 128), BF),
         qy=pltpu.VMEM((2, 2, 4, 16, 128), BF),
-        r3x=pltpu.VMEM((3, 2, 2, 16, 128), BF),
-        r3y=pltpu.VMEM((3, 2, 2, 16, 128), BF),
+        r3x=pltpu.VMEM((2, 3, 2, 16, 128), BF),
+        r3y=pltpu.VMEM((2, 3, 2, 16, 128), BF),
         t=pltpu.VMEM((4, 2, 16, 128), BF),
         r4=pltpu.VMEM(last, BF),
     )
@@ -63,8 +63,8 @@
     )
 
 
-N_RECV = 52
-N_SEND = 66
+N_RECV = 79
+N_SEND = 79
 
 SCRATCH = dict(
     arr=pltpu.VMEM((T, 4096), BF),
@@ -82,8 +82,10 @@
     ss=pltpu.VMEM((32, 128), BF),
     bc=pltpu.VMEM((8, 32, 128), BF),
     norm=pltpu.VMEM((8, 8, 128), F32),
-    dbcs=pltpu.VMEM((8, 32, 128), F32),
-    dbcr=pltpu.VMEM((8, 32, 128), F32),
+    dbcs=pltpu.VMEM((8, 32, 128), BF),
+    dbcr=pltpu.VMEM((8, 32, 128), BF),
+    dsum=pltpu.VMEM((32, 128), F32),
+    dgot=pltpu.VMEM((32, 128), F32),
     dx=pltpu.VMEM((4, 128, 128), BF),
     dz=pltpu.VMEM((4, 128, 128), BF),
     nm=pltpu.VMEM((4, 128, 128), BF),
@@ -167,9 +169,9 @@
     for head, mb in peers:
         pl.semaphore_signal(barrier, inc=1, device_id=(head, mb), device_id_type=MESH)
         count += 1
-    own_parts = [4 * g + k for k in range(4)] + [32 + 4 * g + k for k in range(4)]
-    targets = [8 * g_t + k for k in range(8)]
-    for head in own_parts + targets:
+    target = 8 * g_t + part
+    source = 4 * g + j + 28 * (j // 4)
+    for head in (target, source):
         pl.semaphore_signal(barrier, inc=1, device_id=(head, m), device_id_type=MESH)
         count += 1
 
@@ -206,39 +208,37 @@
             value = lax.select(pick, v, value)
         return value
 
-    def stage1_copies(b):
-        return [([(b["p"].at[:, :, 1 - c], b["r1"], head_of(zh, x, y, 1 - c), m)], b["r1"])]
-
-    def stage1_merge(b, picks):
-        def one(q, _):
+    def stage1_copies(b, k):
+        head = head_of(zh, x, y, 1 - c)
+        return [([(b["p"].at[q, :, 1 - c], b["r1"].at[q], head, m) for q in (k, 2 + k)], b["r1"].at[0:2])]
+
+    def stage1_merge(b, k, picks):
+        for q in (k, 2 + k):
             b["q"][q] = combine(b["p"][q, :, c], [b["r1"][q]], picks and picks["c"]).astype(BF)
-            return 0
-        lax.fori_loop(0, 4, one, 0)
-
-    def stage2_copies(b):
+
+    def stage2_copies(b, k):
         along_x, along_y = [], []
         for d in range(1, 4):
             x2, y2 = (x + d) % 4, (y + d) % 4
-            along_x.append((b["q"].at[0:2, :, :, x2], b["r2x"].at[d - 1], head_of(zh, x2, y, c), m))
-            along_y.append((b["q"].at[2:4, y2], b["r2y"].at[d - 1], head_of(zh, x, y2, c), m))
-        return [(along_x, b["r2x"]), (along_y, b["r2y"])]
-
-    def stage2_merge(b, picks):
-        for q in range(2):
-            b["qx"][q] = combine(b["q"][q, :, :, x], [b["r2x"][d, q] for d in range(3)], picks and picks["x"]).astype(BF)
-            b["qy"][q] = combine(b["q"][2 + q, y], [b["r2y"][d, q] for d in range(3)], picks and picks["y"]).astype(BF)
-
-    def stage3_copies(b):
+            along_x.append((b["q"].at[k, :, :, x2], b["r2x"].at[k, d - 1], head_of(zh, x2, y, c), m))
+            along_y.append((b["q"].at[2 + k, y2], b["r2y"].at[k, d - 1], head_of(zh, x, y2, c), m))
+        return [(along_x, b["r2x"].at[k]), (along_y, b["r2y"].at[k])]
+
+    def stage2_merge(b, k, picks):
+        b["qx"][k] = combine(b["q"][k, :, :, x], [b["r2x"][k, d] for d in range(3)], picks and picks["x"]).astype(BF)
+        b["qy"][k] = combine(b["q"][2 + k, y], [b["r2y"][k, d] for d in range(3)], picks and picks["y"]).astype(BF)
+
+    def stage3_copies(b, k):
         along_x, along_y = [], []
         for d in range(1, 4):
             x2, y2 = (x + d) % 4, (y + d) % 4
-            along_y.append((b["qx"].at[:, y2], b["r3x"].at[d - 1], head_of(zh, x, y2, c), m))
-            along_x.append((b["qy"].at[:, :, x2], b["r3y"].at[d - 1], head_of(zh, x2, y, c), m))
-        return [(along_y, b["r3x"]), (along_x, b["r3y"])]
-
-    def stage3_merge(b, picks):
-        b["t"][0:2] = combine(b["qx"][:, y], [b["r3x"][d] for d in range(3)], picks and picks["y"]).astype(BF)
-        b["t"][2:4] = combine(b["qy"][:, :, x], [b["r3y"][d] for d in range(3)], picks and picks["x"]).astype(BF)
+            along_y.append((b["qx"].at[k, y2], b["r3x"].at[k, d - 1], head_of(zh, x, y2, c), m))
+            along_x.append((b["qy"].at[k, :, x2], b["r3y"].at[k, d - 1], head_of(zh, x2, y, c), m))
+        return [(along_y, b["r3x"].at[k]), (along_x, b["r3y"].at[k])]
+
+    def stage3_merge(b, k, picks):
+        b["t"][k] = combine(b["qx"][k, y], [b["r3x"][k, d] for d in range(3)], picks and picks["y"]).astype(BF)
+        b["t"][2 + k] = combine(b["qy"][k, :, x], [b["r3y"][k, d] for d in range(3)], picks and picks["x"]).astype(BF)
 
     other_zh = head_of(1 - zh, x, y, c)
 
@@ -294,16 +294,18 @@
         y=[o_y == (y + 4 - d) % 4 for d in range(1, 4)],
     )
     a_x, a_o = s["ax"], s["ao"]
-    x1 = go(stage1_copies(sx))
+    x1 = [go(stage1_copies(sx, k)) for k in range(2)]
     tog = s["tog"]
     og = og_ref[...].astype(F32)
     for k in range(8):
         for q in range(4):
             tog["g"][k * 8 + q * 2:k * 8 + q * 2 + 2, :] = og[:, q * 1024 + k * 128:q * 1024 + k * 128 + 128]
     o1 = go(trade(tog))
-    got(x1)
-    stage1_merge(sx, picks)
-    x2 = go(stage2_copies(sx))
+    x2 = []
+    for k in range(2):
+        got(x1[k])
+        stage1_merge(sx, k, picks)
+        x2.append(go(stage2_copies(sx, k)))
     got(o1)
     for q in range(4):
         for tt in range(2):
@@ -318,24 +320,33 @@
     oz = go([([(oz_ref, oz_ref, other_zh, m)], oz_ref)])
     loc[1].wait()
     unpack_weights(0, 3)
-    got(x2)
-    stage2_merge(sx, picks)
-    x3 = go(stage3_copies(sx))
+    x3 = []
+    for k in range(2):
+        got(x2[k])
+        stage2_merge(sx, k, picks)
+        x3.append(go(stage3_copies(sx, k)))
     got(oz)
     q01, q23 = slice(0, 2), slice(2, 4)
     og1 = go(gather1(a_o, q01, q23))
     unpack_weights(3, 6)
-    got(x3)
-    stage3_merge(sx, picks)
-    x4 = go([([(sx["t"], sx["r4"], other_zh, m)], sx["r4"])])
+    x4 = []
+    for k in range(2):
+        got(x3[k])
+        stage3_merge(sx, k, picks)
+        x4.append(go([([(sx["t"].at[q], sx["r4"].at[q], other_zh, m) for q in (k, 2 + k)], sx["r4"].at[0:2])]))
     got(oc)
     ocz_ref = a_o.at[4:7, y, c, zh, x]
     ocz = go([([(ocz_ref, ocz_ref, other_zh, m)], ocz_ref)])
     got(og1)
     unpack_weights(6, 9)
-    got(x4)
-    a_x[0:4, y, c, :, x] = combine(sx["t"][...], [sx["r4"][...]], [o_zh != zh])
-    xg1 = go(gather1(a_x, q01, q23))
+    xg1, xg2, xg3 = [], [], []
+    first = [slice(k, k + 1) for k in range(2)]
+    second = [slice(2 + k, 3 + k) for k in range(2)]
+    for k in range(2):
+        got(x4[k])
+        for q in (k, 2 + k):
+            a_x[q, y, c, :, x] = combine(sx["t"][q], [sx["r4"][q]], [o_zh != zh])
+        xg1.append(go(gather1(a_x, first[k], second[k])))
     cps = []
     for d in range(1, 4):
         m2 = (m + d) % 4
@@ -344,28 +355,36 @@
     k1, k2 = slice(4, 5), slice(5, 7)
     l1, l2 = slice(4, 6), slice(6, 7)
     unpack_weights(9, 12)
-    got(xg1)
-    xg2 = go(gather2(a_x, q01, q23))
+    for k in range(2):
+        got(xg1[k])
+        xg2.append(go(gather2(a_x, first[k], second[k])))
     got(ocz)
     cog1 = go(gather1(a_o, l1, l2))
     got(xc)
     cxg1 = go(gather1(a_x, k1, k2))
     unpack_weights(12, 16)
-    got(xg2)
-    xg3 = go(gather3(a_x, slice(0, 4)))
+    for k in range(2):
+        got(xg2[k])
+        xg3.append(go(gather3(a_x, first[k]) + gather3(a_x, second[k])))
     og2 = go(gather2(a_o, q01, q23))
 
-    def assemble(a, dst, cc):
+    def assemble(a, dst, cc, q):
         def one(i, _):
-            at = pl.ds(pl.multiple_of(i * 256 + cc * 128, 128), 128)
-            dst[:, at] = a[i // 4, i % 4, cc].reshape(128, 128)
+            at = pl.ds(pl.multiple_of(q * 1024 + i * 256 + cc * 128, 128), 128)
+            dst[:, at] = a[q, i, cc].reshape(128, 128)
             return 0
-        lax.fori_loop(0, 16, one, 0, unroll=8)
-
-    assemble(a_x, s["x"], c)
+        lax.fori_loop(0, 4, one, 0, unroll=True)
+
+    for q in range(4):
+        assemble(a_x, s["x"], c, q)
     loc[2].wait()
-    got(xg3)
-    assemble(a_x, s["x"], 1 - c)
+    p2 = jnp.zeros((T, 128), F32)
+    for k in range(2):
+        got(xg3[k])
+        for q in (k, 2 + k):
+            assemble(a_x, s["x"], 1 - c, q)
+            at = slice(q * 1024, (q + 1) * 1024)
+            p2 = p2 + bdot(s["x"][:, at], s["w2"][:, at], NT)
 
     e1 = doc_ref[0, 0]
     e2 = e1 + doc_ref[0, 1]
@@ -391,22 +410,23 @@
             result = result + pltpu.roll(jnp.where(same[o], d, 0.0), T - o, 0) * taps[3 - o:4 - o]
         return result
 
-    p2 = bdot(s["x"][...], s["w2"][...], NT)
     taps_bc = s["cbc"][...]
     bc_pre = conv(p2, taps_bc)
     bc_sig = sigmoid(bc_pre)
     s["ss"][...] = jnp.transpose(bc_pre * bc_sig)[0:32].astype(BF)
-    i_bc, r_bc = sids.take(8), rids.take(1)
-    for k in range(8):
-        head = 8 * g_t + k
-
-        @pl.when(head != h)
-        def _():
-            copy(s["ss"], s["bc"].at[part], i_bc + k, r_bc, head, m).start()
-
-        @pl.when(head == h)
-        def _():
-            pltpu.make_async_copy(s["ss"], s["bc"].at[part], rsem.at[r_bc]).start()
+    i_bc, r_bc = sids.take(1), rids.take(1)
+
+    @pl.when(target != h)
+    def _():
+        copy(s["ss"], s["bc"].at[part], i_bc, r_bc, target, m).start()
+
+    @pl.when(target == h)
+    def _():
+        pltpu.make_async_copy(s["ss"], s["bc"].at[part], rsem.at[r_bc]).start()
+
+    wait_all(s["bc"].at[j], rsem.at[r_bc])
+    peers_of = [8 * g + (j + d) % 8 for d in range(1, 8)]
+    bcp = go([([(s["bc"].at[j], s["bc"].at[j], head, m) for head in peers_of], s["bc"].at[0:7])])
 
     got(cxg1)
     cxg2 = go(gather2(a_x, k1, k2))
@@ -441,13 +461,15 @@
     scaled = x_conv * step
     skip = jnp.where(low, skip_ref[0], skip_ref[1])
 
-    assemble(a_o, s["o"], c)
+    for q in range(4):
+        assemble(a_o, s["o"], c, q)
     got(og3)
-    assemble(a_o, s["o"], 1 - c)
+    for q in range(4):
+        assemble(a_o, s["o"], 1 - c, q)
     loc[3].wait()
     weighted = bdot(s["o"][...], s["wout"][...], NT) * gain_ref[...]
 
-    wait_all(s["bc"], rsem.at[r_bc])
+    got(bcp)
     b_t = s["bc"][0:4].reshape(128, 128)
     c_t = s["bc"][4:8].reshape(128, 128)
     scores = bdot(c_t, b_t, TN)
@@ -460,7 +482,7 @@
     inners = jnp.sum(weighted * gated, axis=1, keepdims=True)
     nmat = jnp.where(lane == 0, squares, jnp.where(lane == 1, inners, 0.0))
     s["norm"][j] = jnp.transpose(nmat)[0:8]
-    cps = [(s["norm"].at[j], s["norm"].at[j], 8 * g + (j + d) % 8, m) for d in range(1, 8)]
+    cps = [(s["norm"].at[j], s["norm"].at[j], head, m) for head in peers_of]
     ncp = go([(cps, s["norm"].at[0:7])])
     got(cxg2)
     cxg3 = go(gather3(a_x, slice(4, 7)))
@@ -481,19 +503,11 @@
     dy0, dy1 = jnp.where(low, d_state, zero), jnp.where(low, zero, d_state)
     d_mix = [hdot(dy0, scaled, NT), hdot(dy1, scaled, NT)]
     d_scores = d_mix[0] * decays[0] + d_mix[1] * decays[1]
-    s["dbcs"][0:4] = hdot(c_t.astype(F32), d_scores, NN).reshape(4, 32, 128)
-    s["dbcs"][4:8] = hdot(b_t.astype(F32), d_scores, NT).reshape(4, 32, 128)
-    i_d, r_d = sids.take(8), rids.take(1)
-    for k in range(8):
-        head = own_parts[k]
-
-        @pl.when(head != h)
-        def _():
-            copy(s["dbcs"].at[k], s["dbcr"].at[j], i_d + k, r_d, head, m).start()
-
-        @pl.when(head == h)
-        def _():
-            pltpu.make_async_copy(s["dbcs"].at[k], s["dbcr"].at[j], rsem.at[r_d]).start()
+    s["dbcs"][0:4] = hdot(c_t.astype(F32), d_scores, NN).reshape(4, 32, 128).astype(BF)
+    s["dbcs"][4:8] = hdot(b_t.astype(F32), d_scores, NT).reshape(4, 32, 128).astype(BF)
+    s["dbcr"][j] = s["dbcs"][j]
+    cps = [(s["dbcs"].at[(j + d) % 8], s["dbcr"].at[j], 8 * g + (j + d) % 8, m) for d in range(1, 8)]
+    dbc = go([(cps, s["dbcr"].at[0:7])])
 
     def to_mb(ref):
         cps = [(ref.at[0], ref.at[4 - d], h, (m + d) % 4) for d in range(1, 4)]
@@ -513,7 +527,19 @@
         lax.fori_loop(0, 16, one, 0, unroll=8)
 
     lo_half(1 - c)
-    lo1 = go(stage1_copies(slo))
+    lo1 = go(stage1_copies(slo, 0) + stage1_copies(slo, 1))
+    got(dbc)
+    s["dsum"][...] = jnp.sum(s["dbcr"][...].astype(F32), axis=0)
+    i_d, r_d = sids.take(1), rids.take(1)
+
+    @pl.when(source != h)
+    def _():
+        copy(s["dsum"], s["dgot"], i_d, r_d, source, m).start()
+
+    @pl.when(source == h)
+    def _():
+        pltpu.make_async_copy(s["dsum"], s["dgot"], rsem.at[r_d]).start()
+
     lo_half(c)
 
     d_scaled = hdot(
@@ -534,12 +560,13 @@
         d_raws.append(d_step * sigmoid(raws[e]))
 
     got(lo1)
-    stage1_merge(slo, None)
-    lo2 = go(stage2_copies(slo))
-
-    wait_all(s["dbcr"], rsem.at[r_d])
+    for k in range(2):
+        stage1_merge(slo, k, None)
+    lo2 = go(stage2_copies(slo, 0) + stage2_copies(slo, 1))
+
+    wait_all(s["dgot"], rsem.at[r_d])
     d_act = jnp.transpose(
-        jnp.concatenate([jnp.sum(s["dbcr"][...], axis=0), jnp.zeros((96, 128), F32)], axis=0)
+        jnp.concatenate([s["dgot"][...], jnp.zeros((96, 128), F32)], axis=0)
     )
     d_bc = conv_back(d_act * (bc_sig * (1.0 + bc_pre * (1.0 - bc_sig))), taps_bc)
     d2 = jnp.where(lane == 32, d_raws[0], jnp.where(lane == 33, d_raws[1], d_bc))
@@ -549,23 +576,29 @@
 
     d_proj = jnp.concatenate([s["dx"][0], s["dz"][0]], axis=1)
 
-    def ig_half(cc):
-        def one(i, _):
-            at = pl.ds(pl.multiple_of(i * 256 + cc * 128, 128), 128)
-            v = bdot(d_proj, s["wxz"][at, :], NT) + bdot(d2_b, s["w2"][:, at], NN)
-            sig["p"][i // 4, i % 4, cc] = v.astype(BF).reshape(2, 4, 16, 128)
-            return 0
-        lax.fori_loop(0, 16, one, 0, unroll=8)
-
-    ig_half(1 - c)
-    ig1 = go(stage1_copies(sig))
-    ig_half(c)
+    def ig_half(cc, k):
+        for q in (k, 2 + k):
+            def one(i, _):
+                at = pl.ds(pl.multiple_of(q * 1024 + i * 256 + cc * 128, 128), 128)
+                v = bdot(d_proj, s["wxz"][at, :], NT) + bdot(d2_b, s["w2"][:, at], NN)
+                sig["p"][q, i, cc] = v.astype(BF).reshape(2, 4, 16, 128)
+                return 0
+            lax.fori_loop(0, 4, one, 0, unroll=True)
+
+    ig1, ig2, ig3, ig4 = [], [], [], []
+    for k in range(2):
+        ig_half(1 - c, k)
+        ig1.append(go(stage1_copies(sig, k)))
+    for k in range(2):
+        ig_half(c, k)
+    for k in range(2):
+        got(ig1[k])
+        stage1_merge(sig, k, None)
+        ig2.append(go(stage2_copies(sig, k)))
     got(lo2)
-    stage2_merge(slo, None)
-    lo3 = go(stage3_copies(slo))
-    got(ig1)
-    stage1_merge(sig, None)
-    ig2 = go(stage2_copies(sig))
+    for k in range(2):
+        stage2_merge(slo, k, None)
+    lo3 = go(stage3_copies(slo, 0) + stage3_copies(slo, 1))
 
     got(n_mb)
     got(cog3)
@@ -581,8 +614,8 @@
 
     lax.fori_loop(0, 8, grad_out, 0, unroll=4)
 
-    def stage4(b):
-        return go([([(b["t"].at[:, 1 - zh], b["r4"], other_zh, m)], b["r4"])])
+    def stage4(b, k):
+        return [([(b["t"].at[q, 1 - zh], b["r4"].at[q], other_zh, m) for q in (k, 2 + k)], b["r4"].at[0:2])]
 
     def stage5(b, t):
         t["v"][...] = (b["t"][:, zh].astype(F32) + b["r4"][...].astype(F32)).reshape(64, 128)
@@ -598,8 +631,9 @@
                 out[:, at:at + 128] = t["r"][k * 8 + q * 2:k * 8 + q * 2 + 2, :].astype(BF)
 
     got(lo3)
-    stage3_merge(slo, None)
-    lo4 = stage4(slo)
+    for k in range(2):
+        stage3_merge(slo, k, None)
+    lo4 = go(stage4(slo, 0) + stage4(slo, 1))
     got(x_mb)
     got(z_mb)
     got(d2_mb)
@@ -625,33 +659,35 @@
         return 0
 
     lax.fori_loop(0, 3, grad_in, 0)
-    got(ig2)
-    stage2_merge(sig, None)
-    ig3 = go(stage3_copies(sig))
+    for k in range(2):
+        got(ig2[k])
+        stage2_merge(sig, k, None)
+        ig3.append(go(stage3_copies(sig, k)))
     lax.fori_loop(3, 5, grad_in, 0)
     got(lo4)
     lo5 = stage5(slo, s["tlo"])
-    got(ig3)
-    stage3_merge(sig, None)
-    ig4 = stage4(sig)
+    for k in range(2):
+        got(ig3[k])
+        stage3_merge(sig, k, None)
+        ig4.append(go(stage4(sig, k)))
     lax.fori_loop(5, 8, grad_in, 0)
     got(lo5)
     finish(s["tlo"], lo_out)
-    got(ig4)
+    for k in range(2):
+        got(ig4[k])
     ig5 = stage5(sig, s["tig"])
     got(ig5)
     finish(s["tig"], ig_out)
 
     for whole, i in sent:
         wait_all(whole, ssem.at[i])
-    for k in range(8):
-        @pl.when(8 * g_t + k != h)
-        def _():
-            wait_all(s["ss"], ssem.at[i_bc + k])
-
-        @pl.when(own_parts[k] != h)
-        def _():
-            wait_all(s["dbcs"].at[k], ssem.at[i_d + k])
+    @pl.when(target != h)
+    def _():
+        wait_all(s["ss"], ssem.at[i_bc])
+
+    @pl.when(source != h)
+    def _():
+        wait_all(s["dsum"], ssem.at[i_d])
 
     assert rids.used <= N_RECV and sids.used <= N_SEND, (rids.used, sids.used)
 

time: 89.4 us -> 89 us (level); the launches traced: 88.1 us -> 88.8 us
  no operation moved by 1% of the time
where the time goes in v3:
time: 89 us; the launch traced here: 88.8 us
  Pallas kernels  87.5 us (98%)
  between operations  1.29 us (1%)
    pallas_call x1, Pallas kernels, per_device(): pl.pallas_call(mixer_kernel, out_shape=shapes, in_specs=[smem] * 5 + [vme...  85.4 us
    pallas_call x1, Pallas kernels, per_device(): pl.pallas_call(place_kernel, out_shape=shapes, in_specs=[vmem] * 6, out_s...  2.11 us

profile of v3, /device:TPU:1, one launch (start us, length us, event | category | flops | bytes accessed | tf_op | source)
XLA Modules:
  0.0 88.8 jit_solution(3099682886409991771)
XLA Ops:
  1.3 85.4 %shard_map.181 = (bf16[2,4096]{1,0:T(2,128)(2,1)}, bf16[2,4096]{1,0:T(2,128)(2,1)}, bf16[2048,128]{1,0:T(8,128)(2,1)}, bf16[32,1024]{1,0:T(8,128)(2,1)}, bf16[2,...) custom-call(s32[1]{0:T(128)S(6)} %copy.20.own_ref, s32[1,4]{1,0:T(1,128)} %doc_ref.1, f32[2]{0:T(128)} %dtb_ref.1, f32[2]{0:T(128)} %alog_ref.1, ...), custom_call_target="tpu_custom_call" | custom-call | tf_op jit(solution)/shard_map/pallas_call | solution.py:712
  86.7 2.1 %shard_map.182 = (bf16[2,4096]{1,0:T(2,128)(2,1)}, bf16[2,4096]{1,0:T(2,128)(2,1)}, bf16[2048,128]{1,0:T(8,128)(2,1)}, bf16[32,1024]{1,0:T(8,128)(2,1)}, bf16[2,...) custom-call(bf16[2,4096]{1,0:T(2,128)(2,1)} %get-tuple-element.18.refs_0_, bf16[2,4096]{1,0:T(2,128)(2,1)} %get-tuple-element.19.refs_1_, ...), custom_call_target="tpu_custom_call" | custom-call | tf_op jit(solution)/shard_map/pallas_call | solution.py:726

commit v4 on v3

--- a/solution.py
+++ b/solution.py
@@ -430,8 +430,6 @@
 
     got(cxg1)
     cxg2 = go(gather2(a_x, k1, k2))
-    got(cog1)
-    cog2 = go(gather2(a_o, l1, l2))
 
     pxz = bdot(s["x"][...], s["wxz"][...], NN)
     got(og2)
@@ -486,8 +484,6 @@
     ncp = go([(cps, s["norm"].at[0:7])])
     got(cxg2)
     cxg3 = go(gather3(a_x, slice(4, 7)))
-    got(cog2)
-    cog3 = go(gather3(a_o, slice(4, 7)))
     got(ncp)
     total = jnp.sum(s["norm"][...], axis=0)
     tcol = jnp.transpose(jnp.concatenate([total, jnp.zeros((120, 128), F32)], axis=0))
@@ -508,6 +504,8 @@
     s["dbcr"][j] = s["dbcs"][j]
     cps = [(s["dbcs"].at[(j + d) % 8], s["dbcr"].at[j], 8 * g + (j + d) % 8, m) for d in range(1, 8)]
     dbc = go([(cps, s["dbcr"].at[0:7])])
+    got(cog1)
+    cog2 = go(gather2(a_o, l1, l2))
 
     def to_mb(ref):
         cps = [(ref.at[0], ref.at[4 - d], h, (m + d) % 4) for d in range(1, 4)]
@@ -565,6 +563,8 @@
     lo2 = go(stage2_copies(slo, 0) + stage2_copies(slo, 1))
 
     wait_all(s["dgot"], rsem.at[r_d])
+    got(cog2)
+    cog3 = go(gather3(a_o, slice(4, 7)))
     d_act = jnp.transpose(
         jnp.concatenate([s["dgot"][...], jnp.zeros((96, 128), F32)], axis=0)
     )
@@ -595,11 +595,6 @@
         got(ig1[k])
         stage1_merge(sig, k, None)
         ig2.append(go(stage2_copies(sig, k)))
-    got(lo2)
-    for k in range(2):
-        stage2_merge(slo, k, None)
-    lo3 = go(stage3_copies(slo, 0) + stage3_copies(slo, 1))
-
     got(n_mb)
     got(cog3)
     nm_all = s["nm"][...].reshape(512, 128)
@@ -630,10 +625,14 @@
                 at = q * 1024 + k * 128
                 out[:, at:at + 128] = t["r"][k * 8 + q * 2:k * 8 + q * 2 + 2, :].astype(BF)
 
-    got(lo3)
-    for k in range(2):
-        stage3_merge(slo, k, None)
-    lo4 = go(stage4(slo, 0) + stage4(slo, 1))
+    for k in range(2):
+        got(ig2[k])
+        stage2_merge(sig, k, None)
+        ig3.append(go(stage3_copies(sig, k)))
+    got(lo2)
+    for k in range(2):
+        stage2_merge(slo, k, None)
+    lo3 = go(stage3_copies(slo, 0) + stage3_copies(slo, 1))
     got(x_mb)
     got(z_mb)
     got(d2_mb)
@@ -658,26 +657,25 @@
         gdt_out[:, at] = small[32:34].astype(BF)
         return 0
 
-    lax.fori_loop(0, 3, grad_in, 0)
-    for k in range(2):
-        got(ig2[k])
-        stage2_merge(sig, k, None)
-        ig3.append(go(stage3_copies(sig, k)))
-    lax.fori_loop(3, 5, grad_in, 0)
-    got(lo4)
-    lo5 = stage5(slo, s["tlo"])
+    lax.fori_loop(0, 4, grad_in, 0)
     for k in range(2):
         got(ig3[k])
         stage3_merge(sig, k, None)
         ig4.append(go(stage4(sig, k)))
-    lax.fori_loop(5, 8, grad_in, 0)
+    got(lo3)
+    for k in range(2):
+        stage3_merge(slo, k, None)
+    lo4 = go(stage4(slo, 0) + stage4(slo, 1))
+    lax.fori_loop(4, 8, grad_in, 0)
+    for k in range(2):
+        got(ig4[k])
+    ig5 = stage5(sig, s["tig"])
+    got(lo4)
+    lo5 = stage5(slo, s["tlo"])
+    got(ig5)
+    finish(s["tig"], ig_out)
     got(lo5)
     finish(s["tlo"], lo_out)
-    for k in range(2):
-        got(ig4[k])
-    ig5 = stage5(sig, s["tig"])
-    got(ig5)
-    finish(s["tig"], ig_out)
 
     for whole, i in sent:
         wait_all(whole, ssem.at[i])

time: 89 us -> 87.9 us (0.988)
  Pallas kernels: 87.5 us -> 86.4 us
    pallas_call x1, Pallas kernels: 85.4 us -> 84.3 us  [per_device(): pl.pallas_call(mixer_kernel, out_shape=shapes, in_specs=[smem] * 5 + [vme...]
where the time goes in v4:
time: 87.9 us; the launch traced here: 87.7 us
  Pallas kernels  86.4 us (98%)
  between operations  1.29 us (1%)
    pallas_call x1, Pallas kernels, per_device(): pl.pallas_call(mixer_kernel, out_shape=shapes, in_specs=[smem] * 5 + [vme...  84.3 us
    pallas_call x1, Pallas kernels, per_device(): pl.pallas_call(place_kernel, out_shape=shapes, in_specs=[vmem] * 6, out_s...  2.11 us

profile of v4, /device:TPU:1, one launch (start us, length us, event | category | flops | bytes accessed | tf_op | source)
XLA Modules:
  0.0 87.7 jit_solution(6264363175971679454)
XLA Ops:
  1.3 84.3 %shard_map.181 = (bf16[2,4096]{1,0:T(2,128)(2,1)}, bf16[2,4096]{1,0:T(2,128)(2,1)}, bf16[2048,128]{1,0:T(8,128)(2,1)}, bf16[32,1024]{1,0:T(8,128)(2,1)}, bf16[2,...) custom-call(s32[1]{0:T(128)S(6)} %copy.20.own_ref, s32[1,4]{1,0:T(1,128)} %doc_ref.1, f32[2]{0:T(128)} %dtb_ref.1, f32[2]{0:T(128)} %alog_ref.1, ...), custom_call_target="tpu_custom_call" | custom-call | tf_op jit(solution)/shard_map/pallas_call | solution.py:710
  85.6 2.1 %shard_map.182 = (bf16[2,4096]{1,0:T(2,128)(2,1)}, bf16[2,4096]{1,0:T(2,128)(2,1)}, bf16[2048,128]{1,0:T(8,128)(2,1)}, bf16[32,1024]{1,0:T(8,128)(2,1)}, bf16[2,...) custom-call(bf16[2,4096]{1,0:T(2,128)(2,1)} %get-tuple-element.18.refs_0_, bf16[2,4096]{1,0:T(2,128)(2,1)} %get-tuple-element.19.refs_1_, ...), custom_call_target="tpu_custom_call" | custom-call | tf_op jit(solution)/shard_map/pallas_call | solution.py:724

commit v5 on v4

--- a/solution.py
+++ b/solution.py
@@ -320,24 +320,25 @@
     oz = go([([(oz_ref, oz_ref, other_zh, m)], oz_ref)])
     loc[1].wait()
     unpack_weights(0, 3)
+    got(oz)
+    q01, q23 = slice(0, 2), slice(2, 4)
+    og1 = go(gather1(a_o, q01, q23))
     x3 = []
     for k in range(2):
         got(x2[k])
         stage2_merge(sx, k, picks)
         x3.append(go(stage3_copies(sx, k)))
-    got(oz)
-    q01, q23 = slice(0, 2), slice(2, 4)
-    og1 = go(gather1(a_o, q01, q23))
     unpack_weights(3, 6)
     x4 = []
     for k in range(2):
         got(x3[k])
         stage3_merge(sx, k, picks)
         x4.append(go([([(sx["t"].at[q], sx["r4"].at[q], other_zh, m) for q in (k, 2 + k)], sx["r4"].at[0:2])]))
+    got(og1)
+    og2 = go(gather2(a_o, q01, q23))
     got(oc)
     ocz_ref = a_o.at[4:7, y, c, zh, x]
     ocz = go([([(ocz_ref, ocz_ref, other_zh, m)], ocz_ref)])
-    got(og1)
     unpack_weights(6, 9)
     xg1, xg2, xg3 = [], [], []
     first = [slice(k, k + 1) for k in range(2)]
@@ -354,19 +355,22 @@
     xc = go([(cps, a_x.at[4:7, y, c, :, x])])
     k1, k2 = slice(4, 5), slice(5, 7)
     l1, l2 = slice(4, 6), slice(6, 7)
+    got(ocz)
+    cog1 = go(gather1(a_o, l1, l2))
     unpack_weights(9, 12)
     for k in range(2):
         got(xg1[k])
         xg2.append(go(gather2(a_x, first[k], second[k])))
-    got(ocz)
-    cog1 = go(gather1(a_o, l1, l2))
     got(xc)
     cxg1 = go(gather1(a_x, k1, k2))
+    got(og2)
+    og3 = go(gather3(a_o, slice(0, 4)))
     unpack_weights(12, 16)
     for k in range(2):
         got(xg2[k])
         xg3.append(go(gather3(a_x, first[k]) + gather3(a_x, second[k])))
-    og2 = go(gather2(a_o, q01, q23))
+    got(cog1)
+    cog2 = go(gather2(a_o, l1, l2))
 
     def assemble(a, dst, cc, q):
         def one(i, _):
@@ -430,10 +434,10 @@
 
     got(cxg1)
     cxg2 = go(gather2(a_x, k1, k2))
+    got(cog2)
+    cog3 = go(gather3(a_o, slice(4, 7)))
 
     pxz = bdot(s["x"][...], s["wxz"][...], NN)
-    got(og2)
-    og3 = go(gather3(a_o, slice(0, 4)))
     z = pxz[:, 128:256]
     taps_x = cx_ref[...]
     x_pre = conv(pxz[:, 0:128], taps_x)
@@ -504,8 +508,6 @@
     s["dbcr"][j] = s["dbcs"][j]
     cps = [(s["dbcs"].at[(j + d) % 8], s["dbcr"].at[j], 8 * g + (j + d) % 8, m) for d in range(1, 8)]
     dbc = go([(cps, s["dbcr"].at[0:7])])
-    got(cog1)
-    cog2 = go(gather2(a_o, l1, l2))
 
     def to_mb(ref):
         cps = [(ref.at[0], ref.at[4 - d], h, (m + d) % 4) for d in range(1, 4)]
@@ -563,8 +565,6 @@
     lo2 = go(stage2_copies(slo, 0) + stage2_copies(slo, 1))
 
     wait_all(s["dgot"], rsem.at[r_d])
-    got(cog2)
-    cog3 = go(gather3(a_o, slice(4, 7)))
     d_act = jnp.transpose(
         jnp.concatenate([s["dgot"][...], jnp.zeros((96, 128), F32)], axis=0)
     )

time: 87.9 us -> 89.1 us (1.014)
  Pallas kernels: 86.4 us -> 87.6 us
    pallas_call x1, Pallas kernels: 84.3 us -> 85.5 us  [per_device(): pl.pallas_call(mixer_kernel, out_shape=shapes, in_specs=[smem] * 5 + [vme...]
where the time goes in v5:
time: 89.1 us; the launch traced here: 88.9 us
  Pallas kernels  87.6 us (98%)
  between operations  1.29 us (1%)
    pallas_call x1, Pallas kernels, per_device(): pl.pallas_call(mixer_kernel, out_shape=shapes, in_specs=[smem] * 5 + [vme...  85.5 us
    pallas_call x1, Pallas kernels, per_device(): pl.pallas_call(place_kernel, out_shape=shapes, in_specs=[vmem] * 6, out_s...  2.11 us

profile of v5, /device:TPU:1, one launch (start us, length us, event | category | flops | bytes accessed | tf_op | source)
XLA Modules:
  0.0 88.9 jit_solution(13317995675428410061)
XLA Ops:
  1.3 85.5 %shard_map.181 = (bf16[2,4096]{1,0:T(2,128)(2,1)}, bf16[2,4096]{1,0:T(2,128)(2,1)}, bf16[2048,128]{1,0:T(8,128)(2,1)}, bf16[32,1024]{1,0:T(8,128)(2,1)}, bf16[2,...) custom-call(s32[1]{0:T(128)S(6)} %copy.20.own_ref, s32[1,4]{1,0:T(1,128)} %doc_ref.1, f32[2]{0:T(128)} %dtb_ref.1, f32[2]{0:T(128)} %alog_ref.1, ...), custom_call_target="tpu_custom_call" | custom-call | tf_op jit(solution)/shard_map/pallas_call | solution.py:710
  86.8 2.1 %shard_map.182 = (bf16[2,4096]{1,0:T(2,128)(2,1)}, bf16[2,4096]{1,0:T(2,128)(2,1)}, bf16[2048,128]{1,0:T(8,128)(2,1)}, bf16[32,1024]{1,0:T(8,128)(2,1)}, bf16[2,...) custom-call(bf16[2,4096]{1,0:T(2,128)(2,1)} %get-tuple-element.18.refs_0_, bf16[2,4096]{1,0:T(2,128)(2,1)} %get-tuple-element.19.refs_1_, ...), custom_call_target="tpu_custom_call" | custom-call | tf_op jit(solution)/shard_map/pallas_call | solution.py:724

commit v6 on v4

--- a/solution.py
+++ b/solution.py
@@ -34,8 +34,11 @@
 class Ids:
     def __init__(self):
         self.used = 0
+        self.free = []
 
     def take(self, count):
+        if count == 1 and self.free:
+            return self.free.pop()
         first = self.used
         self.used += count
         return first
@@ -64,7 +67,7 @@
 
 
 N_RECV = 79
-N_SEND = 79
+N_SEND = 48
 
 SCRATCH = dict(
     arr=pltpu.VMEM((T, 4096), BF),
@@ -90,6 +93,8 @@
     dz=pltpu.VMEM((4, 128, 128), BF),
     nm=pltpu.VMEM((4, 128, 128), BF),
     d2=pltpu.VMEM((4, 48, 128), BF),
+    gin=pltpu.VMEM((2048, 128), BF),
+    gout=pltpu.VMEM((1024, 128), BF),
     gf=pltpu.VMEM((2, 256, 128), F32),
     sx=staged((4, 2, 16, 128)),
     slo=staged((4, 16, 128)),
@@ -145,6 +150,12 @@
             sent.append((whole, i))
         return waits
 
+    def flush(mark):
+        for whole, i in [group for group in sent if group[1] < mark]:
+            wait_all(whole, ssem.at[i])
+            sids.free.append(i)
+        sent[:] = [group for group in sent if group[1] >= mark]
+
     def got(waits):
         for whole, r in waits:
             wait_all(whole, rsem.at[r])
@@ -185,13 +196,14 @@
     sx = s["sx"]
     loc[0].wait()
 
-    def split_arr(i, _):
-        v = s["arr"][:, pl.ds(pl.multiple_of(i * 256, 256), 256)]
-        for cc in range(2):
-            sx["p"][i // 4, i % 4, cc] = v[:, cc * 128:(cc + 1) * 128].reshape(2, 4, 16, 128)
-        return 0
-
-    lax.fori_loop(0, 16, split_arr, 0, unroll=4)
+    def split_arr(cc):
+        def one(i, _):
+            v = s["arr"][:, pl.ds(pl.multiple_of(i * 256 + cc * 128, 128), 128)]
+            sx["p"][i // 4, i % 4, cc] = v.reshape(2, 4, 16, 128)
+            return 0
+        lax.fori_loop(0, 16, one, 0, unroll=4)
+
+    split_arr(1 - c)
     pl.semaphore_wait(barrier, count)
 
     owner = own_ref[0]
@@ -295,6 +307,7 @@
     )
     a_x, a_o = s["ax"], s["ao"]
     x1 = [go(stage1_copies(sx, k)) for k in range(2)]
+    split_arr(c)
     tog = s["tog"]
     og = og_ref[...].astype(F32)
     for k in range(8):
@@ -363,6 +376,7 @@
     got(xc)
     cxg1 = go(gather1(a_x, k1, k2))
     unpack_weights(12, 16)
+    mark = sids.used
     for k in range(2):
         got(xg2[k])
         xg3.append(go(gather3(a_x, first[k]) + gather3(a_x, second[k])))
@@ -409,6 +423,8 @@
         for o in range(1, 4):
             result = result + pltpu.roll(jnp.where(same[o], d, 0.0), T - o, 0) * taps[3 - o:4 - o]
         return result
+
+    flush(mark)
 
     taps_bc = s["cbc"][...]
     bc_pre = conv(p2, taps_bc)
@@ -604,10 +620,15 @@
         lhs = jnp.concatenate(
             [a_o[m, yy, cc].reshape(128, 128)] + [a_o[k, yy, cc].reshape(128, 128) for k in range(4, 7)], axis=0
         )
-        go_out[pl.ds(pl.multiple_of(i * 128, 128), 128), :] = bdot(lhs, nm_all, TN).astype(BF)
+        s["gout"][pl.ds(pl.multiple_of(i * 128, 128), 128), :] = bdot(lhs, nm_all, TN).astype(BF)
         return 0
 
     lax.fori_loop(0, 8, grad_out, 0, unroll=4)
+    leave = [
+        pltpu.make_async_copy(s["gout"], go_out, lsem.at[4]),
+        pltpu.make_async_copy(s["gin"], gin_out, lsem.at[5]),
+    ]
+    leave[0].start()
 
     def stage4(b, k):
         return [([(b["t"].at[q, 1 - zh], b["r4"].at[q], other_zh, m) for q in (k, 2 + k)], b["r4"].at[0:2])]
@@ -650,7 +671,7 @@
         r = bdot(lhs, d_all, TN)
         s["gf"][k, pl.ds(0, 128, stride=2), :] = r[:, 0:128]
         s["gf"][k, pl.ds(1, 128, stride=2), :] = r[:, 128:256]
-        gin_out[pl.ds(pl.multiple_of(i * 256, 256), 256), :] = s["gf"][k].astype(BF)
+        s["gin"][pl.ds(pl.multiple_of(i * 256, 256), 256), :] = s["gf"][k].astype(BF)
         small = bdot(d2_all, lhs, NN)
         at = pl.ds(pl.multiple_of(i * 128, 128), 128)
         gbc_out[:, at] = small[0:32].astype(BF)
@@ -667,6 +688,7 @@
         stage3_merge(slo, k, None)
     lo4 = go(stage4(slo, 0) + stage4(slo, 1))
     lax.fori_loop(4, 8, grad_in, 0)
+    leave[1].start()
     for k in range(2):
         got(ig4[k])
     ig5 = stage5(sig, s["tig"])
@@ -677,6 +699,8 @@
     got(lo5)
     finish(s["tlo"], lo_out)
 
+    for cp in leave:
+        cp.wait()
     for whole, i in sent:
         wait_all(whole, ssem.at[i])
     @pl.when(target != h)
@@ -711,7 +735,7 @@
         mixer_kernel,
         out_shape=shapes,
         in_specs=[smem] * 5 + [vmem] * 5 + [hbm] * 4,
-        out_specs=(vmem,) * 6,
+        out_specs=(vmem, vmem, hbm, vmem, vmem, hbm),
         scratch_shapes=[SCRATCH],
         compiler_params=pltpu.CompilerParams(
             collective_id=0, has_side_effects=True, vmem_limit_bytes=56 * 1024 * 1024

time: 87.9 us -> 87.4 us (level)
  no operation moved by 1% of the time
where the time goes in v6:
time: 87.4 us; the launch traced here: 87.3 us
  Pallas kernels  86 us (98%)
  between operations  1.29 us (1%)
    pallas_call x1, Pallas kernels, per_device(): pl.pallas_call(mixer_kernel, out_shape=shapes, in_specs=[smem] * 5 + [vme...  83.9 us
    pallas_call x1, Pallas kernels, per_device(): pl.pallas_call(place_kernel, out_shape=shapes, in_specs=[vmem] * 6, out_s...  2.11 us

profile of v6, /device:TPU:1, one launch (start us, length us, event | category | flops | bytes accessed | tf_op | source)
XLA Modules:
  0.0 87.3 jit_solution(8482859002171146976)
XLA Ops:
  1.3 83.9 %shard_map.181 = (bf16[2,4096]{1,0:T(2,128)(2,1)}, bf16[2,4096]{1,0:T(2,128)(2,1)}, bf16[2048,128]{1,0:T(8,128)(2,1)}, bf16[32,1024]{1,0:T(8,128)(2,1)}, bf16[2,...) custom-call(s32[1]{0:T(128)S(6)} %copy.20.own_ref, s32[1,4]{1,0:T(1,128)} %doc_ref.1, f32[2]{0:T(128)} %dtb_ref.1, f32[2]{0:T(128)} %alog_ref.1, ...), custom_call_target="tpu_custom_call" | custom-call | tf_op jit(solution)/shard_map/pallas_call | solution.py:734
  85.1 2.1 %shard_map.182 = (bf16[2,4096]{1,0:T(2,128)(2,1)}, bf16[2,4096]{1,0:T(2,128)(2,1)}, bf16[2048,128]{1,0:T(8,128)(2,1)}, bf16[32,1024]{1,0:T(8,128)(2,1)}, bf16[2,...) custom-call(bf16[2,4096]{1,0:T(2,128)(2,1)} %get-tuple-element.18.refs_0_, bf16[2,4096]{1,0:T(2,128)(2,1)} %get-tuple-element.19.refs_1_, ...), custom_call_target="tpu_custom_call" | custom-call | tf_op jit(solution)/shard_map/pallas_call | solution.py:748

commit v7 on v6

--- a/solution.py
+++ b/solution.py
@@ -444,8 +444,6 @@
     peers_of = [8 * g + (j + d) % 8 for d in range(1, 8)]
     bcp = go([([(s["bc"].at[j], s["bc"].at[j], head, m) for head in peers_of], s["bc"].at[0:7])])
 
-    got(cxg1)
-    cxg2 = go(gather2(a_x, k1, k2))
 
     pxz = bdot(s["x"][...], s["wxz"][...], NN)
     got(og2)
@@ -498,8 +496,8 @@
     s["norm"][j] = jnp.transpose(nmat)[0:8]
     cps = [(s["norm"].at[j], s["norm"].at[j], head, m) for head in peers_of]
     ncp = go([(cps, s["norm"].at[0:7])])
-    got(cxg2)
-    cxg3 = go(gather3(a_x, slice(4, 7)))
+    got(cxg1)
+    cxg2 = go(gather2(a_x, k1, k2))
     got(ncp)
     total = jnp.sum(s["norm"][...], axis=0)
     tcol = jnp.transpose(jnp.concatenate([total, jnp.zeros((120, 128), F32)], axis=0))
@@ -542,6 +540,8 @@
 
     lo_half(1 - c)
     lo1 = go(stage1_copies(slo, 0) + stage1_copies(slo, 1))
+    got(cxg2)
+    cxg3 = go(gather3(a_x, slice(4, 7)))
     got(dbc)
     s["dsum"][...] = jnp.sum(s["dbcr"][...].astype(F32), axis=0)
     i_d, r_d = sids.take(1), rids.take(1)

time: 87.4 us -> 86.9 us (level)
  no operation moved by 1% of the time
where the time goes in v7:
time: 86.9 us; the launch traced here: 86.8 us
  Pallas kernels  85.5 us (98%)
  between operations  1.29 us (1%)
    pallas_call x1, Pallas kernels, per_device(): pl.pallas_call(mixer_kernel, out_shape=shapes, in_specs=[smem] * 5 + [vme...  83.4 us
    pallas_call x1, Pallas kernels, per_device(): pl.pallas_call(place_kernel, out_shape=shapes, in_specs=[vmem] * 6, out_s...  2.11 us

profile of v7, /device:TPU:1, one launch (start us, length us, event | category | flops | bytes accessed | tf_op | source)
XLA Modules:
  0.0 86.8 jit_solution(9655250867071788051)
XLA Ops:
  1.3 83.4 %shard_map.181 = (bf16[2,4096]{1,0:T(2,128)(2,1)}, bf16[2,4096]{1,0:T(2,128)(2,1)}, bf16[2048,128]{1,0:T(8,128)(2,1)}, bf16[32,1024]{1,0:T(8,128)(2,1)}, bf16[2,...) custom-call(s32[1]{0:T(128)S(6)} %copy.20.own_ref, s32[1,4]{1,0:T(1,128)} %doc_ref.1, f32[2]{0:T(128)} %dtb_ref.1, f32[2]{0:T(128)} %alog_ref.1, ...), custom_call_target="tpu_custom_call" | custom-call | tf_op jit(solution)/shard_map/pallas_call | solution.py:734
  84.7 2.1 %shard_map.182 = (bf16[2,4096]{1,0:T(2,128)(2,1)}, bf16[2,4096]{1,0:T(2,128)(2,1)}, bf16[2048,128]{1,0:T(8,128)(2,1)}, bf16[32,1024]{1,0:T(8,128)(2,1)}, bf16[2,...) custom-call(bf16[2,4096]{1,0:T(2,128)(2,1)} %get-tuple-element.18.refs_0_, bf16[2,4096]{1,0:T(2,128)(2,1)} %get-tuple-element.19.refs_1_, ...), custom_call_target="tpu_custom_call" | custom-call | tf_op jit(solution)/shard_map/pallas_call | solution.py:748
